TPU v7x, 128 devices: a whole 4x4x4 slice. The times are simulated.
128 devices in a mesh: table: 16 (over y, x), col: 8 (over z, core).
Axes of the slice: x: 4, y: 4, z: 4, core: 2. Of those that a mesh axis runs over, the one named last changes fastest.
Arguments:
- table_rows: float32 [32768, 512], P('table', 'col'), may hold values from -6 to 6
- ada_state: float32 [32768], P('table'), may hold values from 0.5 to 20
- w_uvqk: bfloat16 [512, 2048], replicated, may hold values from -0.25 to 0.25
- w_out: bfloat16 [512, 512], replicated, may hold values from -0.25 to 0.25
- tok_owner: int32 [16, 5120, 1], P('table'), may hold values from 0 to 15; in each aligned block of 640 rows (0 to 639, 640 to 1279, ..., all dimensions but the last counted through in order) at most 80 rows name the same one
- tok_slot: int32 [16, 5120], P('table'), may hold values from 0 to 2047
- seg_ids: int32 [128, 640], P(('table', 'col')), may hold values from 0 to 7, never falling along the last dimension, each value on 1 to 160 neighbouring positions
- cotangent: bfloat16 [81920, 512], P(('table', 'col')), may hold values from -60 to 60
Outputs:
- layer_out: bfloat16 [81920, 512], P(('table', 'col'))
- new_table: float32 [32768, 512], P('table', 'col')
- new_state: float32 [32768], P('table')
Inputs may be any that keep to these rules, and one draw needn't show every extreme that they name: `tok_owner`: among the 640 tokens of one device, at most 80 name any one table index. `seg_ids`: along each device's row the sequence numbers never fall; a sequence holds at most 160 tokens.
All inputs are finite; a program needn't handle non-finite values.
Results may differ from a plain program's by a relative error of at most 0.0066.
Values may be sent and summed in bfloat16 or wider, within the bound.
No kernel may reach another device: no remote copies, remote signals or barrier semaphores. Data moves between devices by JAX's collectives and lax.ppermute only.
A program may use at most 128 MiB of HBM per device.

v0:
```python
import jax
import jax.numpy as jnp
from jax import lax
from jax.sharding import PartitionSpec as P

D = 512
HEADS = 4
HDIM = 128
TOK_DEV = 640


NORM_EPS = 1e-05
ROOT_EPS = 1e-08
STEP_SIZE = 0.3


def layer_norm(values):
    center = values - jnp.mean(values, axis=-1, keepdims=True)
    spread = jnp.mean(center * center, axis=-1, keepdims=True)
    return center * lax.rsqrt(spread + NORM_EPS)


def hstu_layer(embedded, segment, w_uvqk, w_out):
    length = embedded.shape[0]
    width = HEADS * HDIM
    resid = embedded.astype(jnp.float32)
    normed = layer_norm(resid).astype(jnp.bfloat16)
    projected = jax.nn.silu(jnp.dot(normed, w_uvqk, preferred_element_type=jnp.float32))
    gates = projected[:, :width]
    values = projected[:, width : 2 * width].astype(jnp.bfloat16).reshape(length, HEADS, HDIM)
    queries = projected[:, 2 * width : 3 * width].astype(jnp.bfloat16).reshape(length, HEADS, HDIM)
    keyset = projected[:, 3 * width :].astype(jnp.bfloat16).reshape(length, HEADS, HDIM)
    scores = jnp.einsum("thd,shd->hts", queries, keyset, preferred_element_type=jnp.float32)
    places = jnp.arange(length)
    allowed = (segment[:, None] == segment[None, :]) & (places[:, None] >= places[None, :])
    weights = jnp.where(allowed[None], jax.nn.silu(scores * HDIM ** (-0.5)), 0.0).astype(
        jnp.bfloat16
    )
    attended = jnp.einsum("hts,shd->thd", weights, values, preferred_element_type=jnp.float32)
    gated = (layer_norm(attended.reshape(length, width)) * gates).astype(jnp.bfloat16)
    return jnp.dot(gated, w_out, preferred_element_type=jnp.float32) + resid


def requests(owner_ids, slot_ids, table_count):
    capacity = TOK_DEV // 8
    tables = jnp.arange(table_count, dtype=jnp.int32)
    owner_hit = (owner_ids[:, None] == tables[None, :]).astype(jnp.float32)
    places = jnp.arange(owner_ids.shape[0], dtype=jnp.int32)
    lower = (places[:, None] >= places[None, :]).astype(jnp.float32)
    running = jnp.dot(lower, owner_hit, precision=lax.Precision.HIGHEST)
    placing = jnp.sum((running - 1.0) * owner_hit, axis=1).astype(jnp.int32)
    flat_index = owner_ids * capacity + placing
    slots = jnp.arange(table_count * capacity, dtype=jnp.int32)
    asking = jnp.sum(jnp.where(flat_index[:, None] == slots[None, :], slot_ids[:, None], 0), axis=0)
    return (flat_index, asking.reshape(table_count, capacity))


def pick_rows(indices, source, block):
    flat = indices.reshape(-1, block)
    columns = jnp.arange(source.shape[0], dtype=jnp.int32)

    def pick_one_block(block_ids):
        onehot = (block_ids[:, None] == columns[None, :]).astype(jnp.bfloat16)
        return jnp.dot(onehot, source, preferred_element_type=jnp.float32).astype(jnp.bfloat16)

    picked = lax.map(pick_one_block, flat)
    return picked.reshape(indices.shape + (source.shape[1],))


def add_rows(indices, incoming, count, block):
    width = incoming.shape[-1]
    flat = indices.reshape(-1, block)
    rows_in = incoming.reshape(-1, block, width)
    columns = jnp.arange(count, dtype=jnp.int32)

    def add_one_block(total, operands):
        block_ids, block_rows = operands
        onehot = (block_ids[:, None] == columns[None, :]).astype(jnp.bfloat16)
        term = lax.dot_general(
            onehot, block_rows, (((0,), (0,)), ((), ())), preferred_element_type=jnp.float32
        )
        return (total + term, None)

    total, _ = lax.scan(add_one_block, jnp.zeros((count, width), jnp.float32), (flat, rows_in))
    return total


def shards(table_rows, ada_state, w_uvqk, w_out, tok_owner, tok_slot, seg_ids, cotangent):
    table_count = lax.axis_size("table")
    col_count = lax.axis_size("col")
    capacity = TOK_DEV // 8
    col_width = table_rows.shape[1]
    member = lax.axis_index("col")
    block = capacity * col_count
    owners_group = tok_owner[0, :, 0].reshape(col_count, TOK_DEV)
    slots_group = tok_slot[0].reshape(col_count, TOK_DEV)
    local_bf = table_rows.astype(jnp.bfloat16)
    own_owner = lax.dynamic_index_in_dim(owners_group, member, 0, keepdims=False)
    own_slot = lax.dynamic_index_in_dim(slots_group, member, 0, keepdims=False)
    flat_index, asking = requests(own_owner, own_slot, table_count)
    spread_ask = jnp.broadcast_to(asking[:, None, :], (table_count, col_count, capacity))
    asked = lax.all_to_all(
        spread_ask.reshape(table_count * col_count, capacity),
        ("table", "col"),
        split_axis=0,
        concat_axis=0,
        tiled=True,
    )
    reply = pick_rows(asked, local_bf, block)
    fetched = lax.all_to_all(reply, ("table", "col"), split_axis=0, concat_axis=0, tiled=True)
    fetched = fetched.reshape(table_count, col_count, capacity, col_width).transpose(0, 2, 1, 3)
    fetched = fetched.reshape(table_count * capacity, D)
    slot_range = jnp.arange(table_count * capacity, dtype=jnp.int32)
    token_onehot = (flat_index[:, None] == slot_range[None, :]).astype(jnp.bfloat16)
    embedded = jnp.dot(token_onehot, fetched, preferred_element_type=jnp.float32).astype(
        jnp.bfloat16
    )
    segment = seg_ids[0]
    result, pullback = jax.vjp(
        lambda rows_in: hstu_layer(rows_in, segment, w_uvqk, w_out), embedded
    )
    (token_grad,) = pullback(cotangent.astype(result.dtype))
    layer_out = result.astype(jnp.bfloat16)
    outgoing = lax.dot_general(
        token_onehot, token_grad, (((0,), (0,)), ((), ())), preferred_element_type=jnp.float32
    ).astype(jnp.bfloat16)
    pieces = outgoing.reshape(table_count, capacity, col_count, col_width).transpose(0, 2, 1, 3)
    pieces = pieces.reshape(table_count * col_count, capacity, col_width)
    arrived = lax.all_to_all(pieces, ("table", "col"), split_axis=0, concat_axis=0, tiled=True)
    row_grad = add_rows(asked, arrived, table_rows.shape[0], block)
    squares = lax.psum(jnp.sum(row_grad * row_grad, axis=1), "col")
    new_state = ada_state + squares / D
    new_table = table_rows - STEP_SIZE * row_grad / (jnp.sqrt(new_state)[:, None] + ROOT_EPS)
    return (layer_out, new_table, new_state)


def solution(mesh):
    in_specs = (
        P("table", "col"),
        P("table"),
        P(),
        P(),
        P("table", None, None),
        P("table", None),
        P(("table", "col"), None),
        P(("table", "col"), None),
    )
    out_specs = (P(("table", "col"), None), P("table", "col"), P("table"))
    return jax.shard_map(shards, mesh=mesh, in_specs=in_specs, out_specs=out_specs, check_vma=False)
```

profile of v0, /device:TPU:1, one launch (start us, length us, event | category | flops | bytes accessed | tf_op | source)
XLA Modules:
  0.0 274.6 jit_solution(1984280654647593910)
XLA Ops:
  5.6 11.5 %all-to-all-start = ((s32[128,1,80]{2,1,0:T(1,128)}), s32[128,1,80]{2,1,0:T(1,128)S(1)}, u32[]{:S(2)}, u32[]{:S(2)}) async-start(s32[128,1,80]{2,1,0:T(1,128)} %bitcast), calls=%async_computation | async-start | bytes 131072 | tf_op jit(solution)/shard_map/all_to_all | solution.py:102
  18.5 8.0 %all-to-all-done = s32[128,1,80]{2,1,0:T(1,128)S(1)} async-done(((s32[128,1,80]{2,1,0:T(1,128)}), s32[128,1,80]{2,1,0:T(1,128)S(1)}, u32[]{:S(2)}, u32[]{:S(2)}) %all-to-all-start) | async-done | bytes 40992 | tf_op jit(solution)/shard_map/all_to_all | solution.py:102
  27.4 30.4 %while.22 = (s32[]{:T(128)}, bf16[16,640,64]{1,2,0:T(8,128)(2,1)}, s32[16,640]{1,0:T(8,128)S(1)}, bf16[2048,64]{1,0:T(8,128)(2,1)S(1)}, s32[]{:T(128)}) while((s32[]{:T(128)}, bf16[16,640,64]{1,2,0:T(8,128)(2,1)}, s32[16,640]{1,0:T(8,128)S(1)}, bf16[2048,64]{1,0:T(8,128)(2,1)S(1)}, s32[]{:T(128)}) %tuple.70), condition=%wide.region_3.4_spmd.clone, body=%wide.region_2.3_spmd.clone.sunk | while | flops 169123840 | bytes 351821 | solution.py:66
  59.8 3.2 %reshape.176 = bf16[128,80,64]{1,0,2:T(8,128)(2,1)} reshape(bf16[16,640,64]{1,0,2:T(8,128)(2,1)S(1)} %copy.97) | data formatting | bytes 2621440 | tf_op jit(solution)/shard_map/reshape | solution.py:67
  63.0 4.2 %copy.98 = bf16[128,80,64]{1,2,0:T(8,128)(2,1)} copy(bf16[128,80,64]{1,0,2:T(8,128)(2,1)} %reshape.176) | data formatting | bytes 2621440 | tf_op jit(solution)/shard_map/reshape | solution.py:67
  67.3 5.8 %all-to-all-start.1 = ((bf16[128,80,64]{1,2,0:T(8,128)(2,1)}), bf16[128,80,64]{1,2,0:T(8,128)(2,1)}, u32[]{:S(2)}, u32[]{:S(2)}) async-start(bf16[128,80,64]{1,2,0:T(8,128)(2,1)} %copy.98), calls=%async_computation.1 | async-start | bytes 4194304 | tf_op jit(solution)/shard_map/all_to_all | solution.py:110
  75.2 27.8 %all-to-all-done.1 = bf16[128,80,64]{1,2,0:T(8,128)(2,1)} async-done(((bf16[128,80,64]{1,2,0:T(8,128)(2,1)}), bf16[128,80,64]{1,2,0:T(8,128)(2,1)}, u32[]{:S(2)}, u32[]{:S(2)}) %all-to-all-start.1) | async-done | bytes 1310752 | tf_op jit(solution)/shard_map/all_to_all | solution.py:110
  103.1 4.2 %copy.144 = bf16[16,8,80,64]{2,0,3,1:T(8,128)(2,1)} copy(bf16[16,8,80,64]{2,3,1,0:T(8,128)(2,1)} %bitcast.1) | data formatting | bytes 2621440 | tf_op jit(solution)/shard_map/reshape | solution.py:111
  107.3 4.5 %reshape.178 = bf16[1280,512]{0,1:T(8,128)(2,1)} reshape(bf16[16,80,8,64]{1,0,3,2:T(8,128)(2,1)} %bitcast.80) | data formatting | bytes 2621440 | tf_op jit(solution)/shard_map/reshape | solution.py:112
  111.9 2.7 convert_reduce_fusion
  114.8 6.2 %fusion.83 = (bf16[640,2048]{1,0:T(8,128)(2,1)S(1)}, f32[640,2048]{1,0:T(8,128)}, f32[640,2048]{1,0:T(8,128)}) fusion(bf16[512,2048]{1,0:T(8,128)(2,1)S(1)} %copy-done, bf16[640,512]{0,1:T(8,128)(2,1)S(1)} %get-tuple-element.142, f32[640]{0:T(1024)S(1)} %fusion.77, f32[640]{0:T(1024)S(1)} %broadcast_multiply_fusion.1), kind=kOutput, calls=%fused_computation.124 | convolution fusion | flops 1350041600 | bytes 15864832 | tf_op jit(solution)/shard_map/jvp()/dot_general | solution.py:28
  124.3 5.8 %select_convert_fusion = (bf16[4,640,640]{2,1,0:T(8,128)(2,1)S(1)}, f32[4,640,640]{2,1,0:T(8,128)}) fusion(pred[640,640]{1,0:T(8,128)(4,1)} %fusion.45, bf16[640,4,128]{0,2,1:T(8,128)(2,1)S(1)} %bitcast.84, bf16[640,4,128]{0,2,1:T(8,128)(2,1)S(1)} %bitcast.82), kind=kOutput, calls=%fused_computation.22 | convolution fusion | flops 430899200 | bytes 11550720 | tf_op jit(solution)/shard_map/jvp(thd,shd->hts)/dot_general | solution.py:33
  134.5 2.3 multiply_reduce_fusion
  136.9 3.1 %fusion.82 = (f32[640]{0:T(1024)S(1)}, f32[640,512]{1,0:T(8,128)S(1)}, f32[640,512]{1,0:T(8,128)}) fusion(f32[640]{0:T(1024)S(1)} %get-tuple-element.139, f32[640,512]{1,0:T(8,128)S(1)} %copy.123, f32[640]{0:T(1024)S(1)} %broadcast_multiply_fusion, f32[640]{0:T(1024)S(1)} %get-tuple-element.140, f32[640,2048]{1,0:T(8,128)} %get-tuple-element.134, ...), kind=kLoop, calls=%fused_computation.123 | loop fusion | flops 3276160 | bytes 5908480 | tf_op jit(solution)/shard_map/transpose(jvp())/reduce_sum | solution.py:18
  140.9 2.2 copy.124
  143.2 3.9 %fusion.86 = bf16[4,128,640]{2,1,0:T(8,128)(2,1)} fusion(bf16[4,128,640]{2,1,0:T(8,128)(2,1)} %bitcast.88, bf16[4,640,640]{2,1,0:T(8,128)(2,1)} %copy-done.1), kind=kOutput, calls=%fused_computation.126 | convolution fusion | flops 419430400 | bytes 4587520 | tf_op jit(solution)/shard_map/transpose(jvp(hts,shd->thd))/dot_general | solution.py:39
  147.1 6.3 %fusion.17 = bf16[4,640,640]{2,1,0:T(8,128)(2,1)S(1)} fusion(f32[4,640,640]{2,1,0:T(8,128)} %get-tuple-element.145, pred[640,640]{1,0:T(8,128)(4,1)S(1)} %copy-done.16, bf16[4,128,640]{2,1,0:T(8,128)(2,1)S(1)} %bitcast.89, bf16[80,4,8,128]{3,2,1,0:T(8,128)(2,1)S(1)} %copy-done.12), kind=kOutput, calls=%fused_computation.21 | convolution fusion | flops 442368000 | bytes 11550720 | tf_op jit(solution)/shard_map/transpose(jvp(hts,shd->thd))/dot_general | solution.py:39
  157.0 2.2 copy.127
  159.2 2.2 copy.125
  163.6 6.3 %fusion.54 = (f32[640]{0:T(1024)S(1)}, bf16[640,512]{0,1:T(8,128)(2,1)S(1)}) fusion(bf16[640,512]{0,1:T(8,128)(2,1)} %copy-done.3, f32[640]{0:T(1024)S(1)} %broadcast_multiply_fusion.1, bf16[512,2048]{1,0:T(8,128)(2,1)S(1)} %copy-done, f32[640,2048]{1,0:T(8,128)} %get-tuple-element.143, f32[640,512]{1,0:T(8,128)} %get-tuple-element.138, ...), kind=kOutput, calls=%fused_computation.74 | convolution fusion | flops 1363803520 | bytes 11932672 | tf_op jit(solution)/shard_map/transpose(jvp())/dot_general | solution.py:28
  170.3 2.5 convolution_convert_fusion
  172.8 2.4 copy.115
  175.3 5.0 %reshape.184 = bf16[16,80,8,64]{1,0,3,2:T(8,128)(2,1)} reshape(bf16[1280,512]{0,1:T(8,128)(2,1)} %copy.115) | data formatting | bytes 2621440 | tf_op jit(solution)/shard_map/reshape | solution.py:127
  180.3 3.5 %copy.116 = bf16[16,8,80,64]{2,3,1,0:T(8,128)(2,1)} copy(bf16[16,8,80,64]{2,0,3,1:T(8,128)(2,1)} %bitcast.81) | data formatting | bytes 2621440 | tf_op jit(solution)/shard_map/transpose | solution.py:127
  183.8 5.8 %all-to-all-start.2 = ((bf16[128,80,64]{1,2,0:T(8,128)(2,1)}), bf16[128,80,64]{1,2,0:T(8,128)(2,1)}, u32[]{:S(2)}, u32[]{:S(2)}) async-start(bf16[128,80,64]{1,2,0:T(8,128)(2,1)} %bitcast.79), calls=%async_computation.2 | async-start | bytes 4194304 | tf_op jit(solution)/shard_map/all_to_all | solution.py:129
  189.6 3.3 %fusion.47 = bf16[640,512]{0,1:T(8,128)(2,1)} fusion(bf16[640,512]{0,1:T(8,128)(2,1)} %copy-done.3, bf16[512,512]{1,0:T(8,128)(2,1)} %param.15, f32[640,2048]{1,0:T(8,128)} %get-tuple-element.134, f32[640,512]{1,0:T(8,128)S(1)} %copy.123, f32[640]{0:T(1024)S(1)} %get-tuple-element.140, f32[640]{0:T(1024)S(1)} %broadcast_multiply_fusion), kind=kOutput, calls=%fused_computation.65 | convolution fusion | flops 337838080 | bytes 4461568 | tf_op jit(solution)/shard_map/jvp()/dot_general | solution.py:41
  195.0 24.6 %all-to-all-done.2 = bf16[128,80,64]{1,2,0:T(8,128)(2,1)} async-done(((bf16[128,80,64]{1,2,0:T(8,128)(2,1)}), bf16[128,80,64]{1,2,0:T(8,128)(2,1)}, u32[]{:S(2)}, u32[]{:S(2)}) %all-to-all-start.2) | async-done | bytes 1310752 | tf_op jit(solution)/shard_map/all_to_all | solution.py:129
  219.6 4.3 %copy.128 = bf16[128,80,64]{2,1,0:T(8,128)(2,1)} copy(bf16[128,80,64]{1,2,0:T(8,128)(2,1)} %all-to-all-done.2) | data formatting | bytes 2621440
  223.9 35.9 %while.23 = (s32[]{:T(128)}, f32[2048,64]{0,1:T(8,128)S(1)}, s32[16,640]{1,0:T(8,128)S(1)}, bf16[16,640,64]{2,1,0:T(8,128)(2,1)}, s32[]{:T(128)}, /*index=5*/s32[]{:T(128)}) while((s32[]{:T(128)}, f32[2048,64]{0,1:T(8,128)S(1)}, s32[16,640]{1,0:T(8,128)S(1)}, bf16[16,640,64]{2,1,0:T(8,128)(2,1)}, s32[]{:T(128)}, ...), condition=%wide.region_13.14_spmd.clone, body=%wide.region_12.13_spmd.clone.sunk | while | flops 169345024 | bytes 1220191 | solution.py:84
  223.9 2.2 fusion.113
  235.2 2.2 fusion.113
  259.9 13.2 %psum.7 = f32[2048]{0:T(1024)S(1)} all-reduce(f32[2048]{0:T(1024)S(1)} %multiply_reduce_fusion.1), channel_id=1, replica_groups=mesh['table'=16,'col'=8] {'col'}, use_global_device_ids=true, to_apply=%region_15.16 | all-reduce | flops 2048 | bytes 16384 | tf_op jit(solution)/shard_map/psum | solution.py:131
  (143 shorter events, 91.5 us)
Async XLA Ops:
  0.6 114.1 %copy-start = (bf16[512,2048]{1,0:T(8,128)(2,1)S(1)}, bf16[512,2048]{1,0:T(8,128)(2,1)}, u32[]{:S(2)}) copy-start(bf16[512,2048]{1,0:T(8,128)(2,1)} %param.14) | copy-start | bytes 6291460
  5.6 20.8 %all-to-all-start = ((s32[128,1,80]{2,1,0:T(1,128)}), s32[128,1,80]{2,1,0:T(1,128)S(1)}, u32[]{:S(2)}, u32[]{:S(2)}) async-start(s32[128,1,80]{2,1,0:T(1,128)} %bitcast), calls=%async_computation | async-start | bytes 131072 | tf_op jit(solution)/shard_map/all_to_all | solution.py:102
  67.2 5.8 %copy-start.18 = (s32[1,640]{1,0:T(1,128)S(1)}, s32[1,640]{1,0:T(1,128)}, u32[]{:S(2)}) copy-start(s32[1,640]{1,0:T(1,128)} %param.18) | copy-start | bytes 7684
  67.3 5.9 %copy-start.5 = (bf16[640,512]{1,0:T(8,128)(2,1)S(1)}, bf16[640,512]{1,0:T(8,128)(2,1)}, u32[]{:S(2)}) copy-start(bf16[640,512]{1,0:T(8,128)(2,1)} %param.19) | copy-start | bytes 1966084
  67.3 35.8 %all-to-all-start.1 = ((bf16[128,80,64]{1,2,0:T(8,128)(2,1)}), bf16[128,80,64]{1,2,0:T(8,128)(2,1)}, u32[]{:S(2)}, u32[]{:S(2)}) async-start(bf16[128,80,64]{1,2,0:T(8,128)(2,1)} %copy.98), calls=%async_computation.1 | async-start | bytes 4194304 | tf_op jit(solution)/shard_map/all_to_all | solution.py:110
  114.5 6.5 %copy-start.3 = (bf16[640,512]{0,1:T(8,128)(2,1)}, bf16[640,512]{0,1:T(8,128)(2,1)S(1)}, u32[]{:S(2)}) copy-start(bf16[640,512]{0,1:T(8,128)(2,1)S(1)} %get-tuple-element.142) | copy-start | bytes 1966084
  122.6 7.4 %copy-start.6 = (bf16[640,512]{0,1:T(8,128)(2,1)}, bf16[640,512]{0,1:T(8,128)(2,1)S(1)}, u32[]{:S(2)}) copy-start(bf16[640,512]{0,1:T(8,128)(2,1)S(1)} %copy.131) | copy-start | bytes 1966084
  124.2 5.8 %copy-start.8 = (bf16[640,512]{0,1:T(8,128)(2,1)}, bf16[640,512]{0,1:T(8,128)(2,1)S(1)}, u32[]{:S(2)}) copy-start(bf16[640,512]{0,1:T(8,128)(2,1)S(1)} %copy.130) | copy-start | bytes 1966084
  124.3 5.8 %copy-start.11 = (bf16[80,4,8,128]{3,2,1,0:T(8,128)(2,1)S(1)}, bf16[80,4,8,128]{3,2,1,0:T(8,128)(2,1)}, u32[]{:S(2)}) copy-start(bf16[80,4,8,128]{3,2,1,0:T(8,128)(2,1)} %get-tuple-element.135) | copy-start | bytes 1966084
  130.0 1.7 copy-start.1
  131.7 1.1 copy-start.2
  143.2 3.9 %copy-start.10 = (bf16[640,512]{0,1:T(8,128)(2,1)S(1)}, bf16[640,512]{0,1:T(8,128)(2,1)}, u32[]{:S(2)}) copy-start(bf16[640,512]{0,1:T(8,128)(2,1)} %copy.124) | copy-start | bytes 1966084
  143.2 3.9 %copy-start.12 = (bf16[80,4,8,128]{3,2,1,0:T(8,128)(2,1)S(1)}, bf16[80,4,8,128]{3,2,1,0:T(8,128)(2,1)}, u32[]{:S(2)}) copy-start(bf16[80,4,8,128]{3,2,1,0:T(8,128)(2,1)} %get-tuple-element.135) | copy-start | bytes 1966084
  143.2 3.9 %copy-start.16 = (pred[640,640]{1,0:T(8,128)(4,1)S(1)}, pred[640,640]{1,0:T(8,128)(4,1)}, u32[]{:S(2)}) copy-start(pred[640,640]{1,0:T(8,128)(4,1)} %fusion.45) | copy-start | bytes 1228804
  147.0 6.3 %copy-start.7 = (bf16[640,512]{0,1:T(8,128)(2,1)S(1)}, bf16[640,512]{0,1:T(8,128)(2,1)}, u32[]{:S(2)}) copy-start(bf16[640,512]{0,1:T(8,128)(2,1)} %copy-done.6) | copy-start | bytes 1966084
  153.4 2.0 copy-start.9
  163.6 6.4 %copy-start.4 = (bf16[640,512]{0,1:T(8,128)(2,1)S(1)}, bf16[640,512]{0,1:T(8,128)(2,1)}, u32[]{:S(2)}) copy-start(bf16[640,512]{0,1:T(8,128)(2,1)} %copy-done.3) | copy-start | bytes 1966084
  163.6 6.7 %copy-start.15 = (bf16[640,512]{0,1:T(8,128)(2,1)S(1)}, bf16[640,512]{0,1:T(8,128)(2,1)}, u32[]{:S(2)}) copy-start(bf16[640,512]{0,1:T(8,128)(2,1)} %copy.105) | copy-start | bytes 1966084
  183.8 35.8 %all-to-all-start.2 = ((bf16[128,80,64]{1,2,0:T(8,128)(2,1)}), bf16[128,80,64]{1,2,0:T(8,128)(2,1)}, u32[]{:S(2)}, u32[]{:S(2)}) async-start(bf16[128,80,64]{1,2,0:T(8,128)(2,1)} %bitcast.79), calls=%async_computation.2 | async-start | bytes 4194304 | tf_op jit(solution)/shard_map/all_to_all | solution.py:129
  195.0 28.9 %copy-start.14 = (f32[2048,64]{0,1:T(8,128)S(1)}, f32[2048,64]{0,1:T(8,128)}, u32[]{:S(2)}) copy-start(f32[2048,64]{0,1:T(8,128)} %custom-call) | copy-start | bytes 1572868
  223.9 49.3 %copy-start.17 = (f32[2048]{0:T(1024)S(1)}, f32[2048]{0:T(1024)}, u32[]{:S(2)}) copy-start(f32[2048]{0:T(1024)} %param.13) | copy-start | bytes 24580
  223.9 49.9 %copy-start.13 = (f32[2048,64]{0,1:T(8,128)S(1)}, f32[2048,64]{0,1:T(8,128)}, u32[]{:S(2)}) copy-start(f32[2048,64]{0,1:T(8,128)} %param.12) | copy-start | bytes 1572868
where the time goes:
time: 276 us; the launch traced here: 275 us
  matrix products  109 us (39%)
  waiting for transfers between devices  60.4 us (22%)
  local copies, waits for them, and re-layouts  55.2 us (20%)
  starting transfers between devices  23.1 us (8%)
  blocking collectives  13.2 us (5%)
  other arithmetic  11.6 us (4%)
    dot_general x16, matrix products, add_one_block(): lax.dot_general(onehot, block_rows, (((0,), (0,)), ((), ())), preferred_e...  35.1 us
    dot_general x16, matrix products, pick_one_block(): jnp.dot(onehot, source, preferred_element_type=jnp.float32)  30 us
    all_to_all x1, waiting for transfers between devices, shards(): lax.all_to_all(reply, ('table', 'col'), split_axis=0, concat_axis=0, tile...  27.8 us
    all_to_all x1, waiting for transfers between devices, shards(): lax.all_to_all(pieces, ('table', 'col'), split_axis=0, concat_axis=0, til...  24.6 us
    psum x1, blocking collectives, shards(): squares = lax.psum(jnp.sum(row_grad * row_grad, axis=1), 'col')  13.2 us
    dot_general x2, matrix products, hstu_layer(): jnp.dot(normed, w_uvqk, preferred_element_type=jnp.float32)  12.6 us
    unnamed x44, local copies, waits for them, and re-layouts  12.2 us
    all_to_all x1, starting transfers between devices, shards(): lax.all_to_all(spread_ask.reshape(table_count * col_count, capacity), ('t...  11.5 us
  transfers between devices with their start and end apart: 3, of which 3 were waited for; matrix products, arithmetic and copies ran while one was open for 3% of the time, Pallas kernels for 0%

commit v1 on v0

v1 whole, which is shorter than its diff:
```python
import functools

import jax
import jax.numpy as jnp
from jax import lax
from jax.experimental import pallas as pl
from jax.experimental.pallas import tpu as pltpu
from jax.sharding import PartitionSpec as P

D = 512
HEADS = 4
HDIM = 128
TOK_DEV = 640
TABLES = 16
COLS = 8
CAP = 80
HALF = CAP // 2
TOUCH = 2048
WIDTH = D // COLS
HI = 256
HI_BITS = 8
LO = TOUCH // HI
ASKS = 768
BLOCK = 128
MAXLEN = 160

NORM_EPS = 1e-05
ROOT_EPS = 1e-08
STEP_SIZE = 0.3

F32 = jnp.float32
BF16 = jnp.bfloat16
I32 = jnp.int32
VMEM_BYTES = 48 * 1024 * 1024


def iota(shape, dim):
    return lax.broadcasted_iota(I32, shape, dim)


def nt_dot(a, b):
    return lax.dot_general(a, b, (((1,), (1,)), ((), ())), preferred_element_type=F32)


def tn_dot(a, b):
    return lax.dot_general(a, b, (((0,), (0,)), ((), ())), preferred_element_type=F32)


def params():
    return pltpu.CompilerParams(vmem_limit_bytes=VMEM_BYTES)


def ask_kernel(owner_ref, slot_ref, asks_ref, place_ref):
    lower = jnp.where(iota((TOK_DEV, TOK_DEV), 0) <= iota((TOK_DEV, TOK_DEV), 1), 1.0, 0.0).astype(BF16)
    table = iota((TABLES, TOK_DEV), 0)
    spans = [slice(TOK_DEV * m, TOK_DEV * (m + 1)) for m in range(COLS)]
    hits = [jnp.where(owner_ref[:, span] == table, 1.0, 0.0) for span in spans]
    running = jnp.dot(
        jnp.concatenate(hits, axis=0).astype(BF16), lower, preferred_element_type=F32
    )
    lane = iota((TABLES, 128), 1)
    slot_at = iota((128, TOK_DEV), 0)
    tiles = [jnp.zeros((TABLES, 128), F32) for _ in range(ASKS // 128)]
    for m, span in enumerate(spans):
        count = running[TABLES * m : TABLES * (m + 1)] * hits[m]
        placing = jnp.sum(count, axis=0, keepdims=True).astype(I32) - 1
        onehot = jnp.where(slot_at == placing, 1.0, 0.0).astype(BF16)
        slot = slot_ref[:, span]
        high = (slot >> HI_BITS).astype(F32) * hits[m]
        low = (slot & (HI - 1)).astype(F32) * hits[m]
        found = nt_dot(jnp.concatenate([high, low], axis=0).astype(BF16), onehot)
        value = found[:TABLES] * float(HI) + found[TABLES:]
        for h in range(2):
            begin = h * (ASKS // 2) + m * HALF
            moved = pltpu.roll(value, (begin - h * HALF) % 128, 1)
            for j in range(begin // 128, (begin + HALF - 1) // 128 + 1):
                at = lane + 128 * j
                tiles[j] = jnp.where((at >= begin) & (at < begin + HALF), moved, tiles[j])
        place_ref[m : m + 1, :] = (
            owner_ref[:, span] * HALF
            + placing
            + jnp.where(placing >= HALF, TABLES * HALF - HALF, 0)
        )
    for j, tile in enumerate(tiles):
        asks_ref[:, 0, 128 * j : 128 * (j + 1)] = tile.astype(I32)


def make_asks(owner, slot):
    return pl.pallas_call(
        ask_kernel,
        out_shape=(
            jax.ShapeDtypeStruct((TABLES, 1, ASKS), I32),
            jax.ShapeDtypeStruct((COLS, TOK_DEV), I32),
        ),
        compiler_params=params(),
        name="ask",
    )(owner, slot)


def ask_onehot(ask):
    return jnp.where(iota((HI, ASKS), 0) == (ask & (HI - 1)), 1.0, 0.0).astype(BF16)


def pick_kernel(parity, asks_ref, table_ref, reply_ref, rows_ref):
    par = parity()
    for lo in range(LO):
        rows_ref[WIDTH * lo : WIDTH * (lo + 1), :] = table_ref[:, HI * lo : HI * (lo + 1)].astype(BF16)

    def one_group(g, carry):
        ask = asks_ref[g]
        found = jnp.dot(rows_ref[...], ask_onehot(ask), preferred_element_type=F32)
        low = jnp.broadcast_to(ask >> HI_BITS, (WIDTH, ASKS))
        kept = found[:WIDTH]
        for lo in range(1, LO):
            kept = jnp.where(low == lo, found[WIDTH * lo : WIDTH * (lo + 1)], kept)
        first, second = kept[:, : ASKS // 2], kept[:, ASKS // 2 :]
        stacked = jnp.concatenate(
            [jnp.where(par == 0, first, second), jnp.where(par == 0, second, first)], axis=0
        )
        reply_ref[g] = stacked.T[: COLS * HALF].astype(BF16)
        return carry

    lax.fori_loop(0, TABLES, one_group, 0)


def pick_rows(asks, table_t, parity):
    return pl.pallas_call(
        functools.partial(pick_kernel, parity),
        out_shape=jax.ShapeDtypeStruct((TABLES, COLS * HALF, 128), BF16),
        scratch_shapes=[pltpu.VMEM((LO * WIDTH, HI), BF16)],
        compiler_params=params(),
        name="pick",
    )(asks, table_t)


def add_kernel(parity, asks_ref, arrived_ref, grad_ref, squares_ref, total_ref):
    par = parity()
    total_ref[...] = jnp.zeros_like(total_ref)
    empty = jnp.zeros((ASKS // 2 - COLS * HALF, 128), F32)

    def one_group(g, carry):
        ask = asks_ref[g]
        block = jnp.concatenate([arrived_ref[g].astype(F32), empty], axis=0).T
        upper, lower = block[:WIDTH], block[WIDTH:]
        slots = jnp.concatenate(
            [jnp.where(par == 0, upper, lower), jnp.where(par == 0, lower, upper)], axis=1
        )
        low = jnp.broadcast_to(ask >> HI_BITS, (WIDTH, ASKS))
        spread = jnp.concatenate(
            [jnp.where(low == lo, slots, 0.0).astype(BF16) for lo in range(LO)], axis=0
        )
        total_ref[...] += nt_dot(spread, ask_onehot(ask))
        return carry

    lax.fori_loop(0, TABLES, one_group, 0)
    sums = []
    for lo in range(LO):
        part = total_ref[WIDTH * lo : WIDTH * (lo + 1), :]
        grad_ref[:, HI * lo : HI * (lo + 1)] = part
        square = jnp.sum(part * part, axis=0, keepdims=True)
        sums += [square[:, :128], square[:, 128:]]
    squares = jnp.concatenate(sums, axis=0)
    for c in range(COLS):
        squares_ref[c] = squares


def add_rows(asks, arrived, parity):
    return pl.pallas_call(
        functools.partial(add_kernel, parity),
        out_shape=(
            jax.ShapeDtypeStruct((WIDTH, TOUCH), F32),
            jax.ShapeDtypeStruct((COLS, TOUCH // 128, 128), F32),
        ),
        scratch_shapes=[pltpu.VMEM((LO * WIDTH, HI), F32)],
        compiler_params=params(),
        name="add",
    )(asks, arrived)


def update_kernel(squares_ref, state_ref, table_ref, grad_ref, new_table_ref, new_state_ref):
    squares = squares_ref[0]
    for c in range(1, COLS):
        squares = squares + squares_ref[c]
    state = state_ref[...] + squares / D
    new_state_ref[...] = state
    factor = STEP_SIZE / (jnp.sqrt(state) + ROOT_EPS)
    for i in range(TOUCH // 128):
        at = slice(128 * i, 128 * (i + 1))
        new_table_ref[:, at] = table_ref[:, at] - grad_ref[:, at] * factor[i : i + 1]


def update(squares, state, table_t, grad_t):
    return pl.pallas_call(
        update_kernel,
        out_shape=(
            jax.ShapeDtypeStruct((WIDTH, TOUCH), F32),
            jax.ShapeDtypeStruct((TOUCH // 128, 128), F32),
        ),
        compiler_params=params(),
        name="update",
    )(squares, state, table_t, grad_t)


def normalise(values):
    center = values - jnp.mean(values, axis=-1, keepdims=True)
    root = lax.rsqrt(jnp.mean(center * center, axis=-1, keepdims=True) + NORM_EPS)
    return center * root, root


def normalise_back(grad, normed, root):
    along = jnp.mean(grad * normed, axis=-1, keepdims=True)
    return root * (grad - jnp.mean(grad, axis=-1, keepdims=True) - normed * along)


def columns_of(row):
    return jnp.broadcast_to(row.astype(F32), (128, TOK_DEV)).T


def layer_kernel(
    member,
    received_ref,
    place_ref,
    segment_ref,
    w_ref,
    w_out_ref,
    cotangent_ref,
    out_ref,
    pieces_ref,
    slots_ref,
    place_col,
    segment_col,
    embedded_ref,
    normed_ref,
    root_ref,
    gates_ref,
    slope_ref,
    values_ref,
    queries_ref,
    keys_ref,
    grad_u_ref,
    grad_values_ref,
    grad_keys_ref,
    token_grad_ref,
):
    place = place_ref[pl.ds(member(), 1), :]
    place_col[...] = columns_of(place)
    segment_col[...] = columns_of(segment_ref[...])
    left = iota((HALF, 128), 1) < WIDTH
    blocks = TOK_DEV // BLOCK
    four = 4 * HALF

    def gather_slots(t, carry):
        parts = []
        for i in range(4):
            block = received_ref[4 * t + i].astype(F32)
            parts.append([block[HALF * c : HALF * (c + 1)] for c in range(COLS)])
        at = pl.multiple_of(four * t, four)
        for j in range(COLS // 2):
            pairs = [(part[2 * j], part[2 * j + 1]) for part in parts]
            first = [jnp.where(left, even, odd) for even, odd in pairs]
            second = [pltpu.roll(jnp.where(left, odd, even), WIDTH, 1) for even, odd in pairs]
            tile = slice(128 * j, 128 * (j + 1))
            slots_ref[pl.ds(at, four), tile] = jnp.concatenate(first, axis=0).astype(BF16)
            slots_ref[pl.ds(TABLES * HALF + at, four), tile] = jnp.concatenate(second, axis=0).astype(BF16)
        return carry

    lax.fori_loop(0, TABLES // 4, gather_slots, 0)

    def project(b, carry):
        rows = pl.ds(pl.multiple_of(BLOCK * b, BLOCK), BLOCK)
        at = place_col[rows, :].astype(I32)
        lane = iota((BLOCK, 128), 1)
        onehot = jnp.concatenate(
            [jnp.where(at == lane + 128 * j, 1.0, 0.0).astype(BF16) for j in range(TABLES * CAP // 128)],
            axis=1,
        )
        embedded = jnp.dot(onehot, slots_ref[...], preferred_element_type=F32)
        embedded_ref[rows, :] = embedded
        normed, root = normalise(embedded)
        normed = normed.astype(BF16)
        normed_ref[rows, :] = normed
        root_ref[rows, :] = jnp.broadcast_to(root, (BLOCK, 128))
        for j, ref in enumerate((gates_ref, values_ref, queries_ref, keys_ref)):
            part = slice(D * j, D * (j + 1))
            linear = jnp.dot(normed, w_ref[:, part], preferred_element_type=F32)
            gate = 0.5 + 0.5 * jnp.tanh(0.5 * linear)
            swish = linear * gate
            ref[rows, :] = swish.astype(ref.dtype)
            slope_ref[rows, part] = gate + swish * (1.0 - gate)
        return carry

    lax.fori_loop(0, blocks, project, 0)

    grad_values_ref[...] = jnp.zeros_like(grad_values_ref)
    grad_keys_ref[...] = jnp.zeros_like(grad_keys_ref)
    scale = HDIM**-0.5
    for b in range(blocks):
        rows = slice(BLOCK * b, BLOCK * (b + 1))
        begin = max(0, (BLOCK * b - MAXLEN + 1) // BLOCK * BLOCK)
        width = BLOCK * (b + 1) - begin
        span = slice(begin, begin + width)
        segment = jnp.concatenate([segment_col[rows, :]] * (width // 128), axis=1)
        allowed = (segment == segment_ref[:, span].astype(F32)) & (
            iota((BLOCK, width), 0) + (BLOCK * b - begin) >= iota((BLOCK, width), 1)
        )
        saved = []
        attended = []
        for h in range(HEADS):
            head = slice(HDIM * h, HDIM * (h + 1))
            scores = scale * nt_dot(queries_ref[rows, head], keys_ref[span, head])
            gate = 0.5 + 0.5 * jnp.tanh(0.5 * scores)
            swish = scores * gate
            weights = jnp.where(allowed, swish, 0.0).astype(BF16)
            slope = jnp.where(allowed, scale * (gate + swish * (1.0 - gate)), 0.0)
            saved.append((weights, slope))
            attended.append(jnp.dot(weights, values_ref[span, head], preferred_element_type=F32))
        normed, root = normalise(jnp.concatenate(attended, axis=1))
        gates = gates_ref[rows, :]
        gated = (normed * gates).astype(BF16)
        out = jnp.dot(gated, w_out_ref[...], preferred_element_type=F32) + embedded_ref[rows, :]
        out_ref[rows, :] = out.astype(BF16)
        grad_gated = nt_dot(cotangent_ref[rows, :], w_out_ref[...]).astype(BF16).astype(F32)
        grad_u_ref[rows, :D] = (grad_gated * normed * slope_ref[rows, :D]).astype(BF16)
        grad_attended = normalise_back(grad_gated * gates, normed, root).astype(BF16)
        for h in range(HEADS):
            head = slice(HDIM * h, HDIM * (h + 1))
            weights, slope = saved[h]
            grad_weights = nt_dot(grad_attended[:, head], values_ref[span, head])
            grad_scores = (grad_weights * slope).astype(BF16)
            grad_queries = jnp.dot(grad_scores, keys_ref[span, head], preferred_element_type=F32)
            part = slice(2 * D + HDIM * h, 2 * D + HDIM * (h + 1))
            grad_u_ref[rows, part] = (grad_queries * slope_ref[rows, part]).astype(BF16)
            grad_values_ref[span, head] += tn_dot(weights, grad_attended[:, head])
            grad_keys_ref[span, head] += tn_dot(grad_scores, queries_ref[rows, head])

    def project_back(b, carry):
        rows = pl.ds(pl.multiple_of(BLOCK * b, BLOCK), BLOCK)
        grad_u_ref[rows, D : 2 * D] = (grad_values_ref[rows, :] * slope_ref[rows, D : 2 * D]).astype(BF16)
        grad_u_ref[rows, 3 * D :] = (grad_keys_ref[rows, :] * slope_ref[rows, 3 * D :]).astype(BF16)
        grad = nt_dot(grad_u_ref[rows, :], w_ref[...])
        grad = normalise_back(grad, normed_ref[rows, :].astype(F32), root_ref[rows, :1])
        token_grad_ref[rows, :] = (grad + cotangent_ref[rows, :].astype(F32)).astype(BF16)
        return carry

    lax.fori_loop(0, blocks, project_back, 0)

    def send_slots(t, carry):
        halves = []
        for h in range(2):
            onehot = jnp.where(
                place - (TABLES * HALF * h + four * t) == iota((four, TOK_DEV), 0), 1.0, 0.0
            ).astype(BF16)
            halves.append(jnp.dot(onehot, token_grad_ref[...], preferred_element_type=F32))
        for i in range(4):
            parts = []
            for j in range(COLS // 2):
                tile = (slice(HALF * i, HALF * (i + 1)), slice(128 * j, 128 * (j + 1)))
                first, second = halves[0][tile], pltpu.roll(halves[1][tile], WIDTH, 1)
                parts += [jnp.where(left, first, second), jnp.where(left, second, first)]
            pieces_ref[4 * t + i] = jnp.concatenate(parts, axis=0).astype(BF16)
        return carry

    lax.fori_loop(0, TABLES // 4, send_slots, 0)


def layer(received, place, member, segment, w_uvqk, w_out, cotangent):
    return pl.pallas_call(
        functools.partial(layer_kernel, member),
        out_shape=(
            jax.ShapeDtypeStruct((TOK_DEV, D), BF16),
            jax.ShapeDtypeStruct((TABLES, COLS * HALF, 128), BF16),
        ),
        scratch_shapes=[
            pltpu.VMEM((TABLES * CAP, D), BF16),
            pltpu.VMEM((TOK_DEV, 128), F32),
            pltpu.VMEM((TOK_DEV, 128), F32),
            pltpu.VMEM((TOK_DEV, D), F32),
            pltpu.VMEM((TOK_DEV, D), BF16),
            pltpu.VMEM((TOK_DEV, 128), F32),
            pltpu.VMEM((TOK_DEV, D), F32),
            pltpu.VMEM((TOK_DEV, 4 * D), F32),
            pltpu.VMEM((TOK_DEV, D), BF16),
            pltpu.VMEM((TOK_DEV, D), BF16),
            pltpu.VMEM((TOK_DEV, D), BF16),
            pltpu.VMEM((TOK_DEV, 4 * D), BF16),
            pltpu.VMEM((TOK_DEV, D), F32),
            pltpu.VMEM((TOK_DEV, D), F32),
            pltpu.VMEM((TOK_DEV, D), BF16),
        ],
        compiler_params=params(),
        name="layer",
    )(received, place, segment, w_uvqk, w_out, cotangent)


def exchange(blocks):
    blocks = blocks.reshape(TABLES * COLS, HALF, 128)
    blocks = lax.all_to_all(blocks, ("table", "col"), split_axis=0, concat_axis=0, tiled=True)
    return blocks.reshape(TABLES, COLS * HALF, 128)


def shards(table_rows, ada_state, w_uvqk, w_out, tok_owner, tok_slot, seg_ids, cotangent):
    def member():
        return lax.axis_index("col")

    def parity():
        return lax.axis_index("col") % 2

    table_t = table_rows.T
    asks, place = make_asks(tok_owner.reshape(1, COLS * TOK_DEV), tok_slot)
    asked = lax.all_to_all(asks, "table", split_axis=0, concat_axis=0, tiled=True)
    received = exchange(pick_rows(asked, table_t, parity))
    layer_out, pieces = layer(received, place, member, seg_ids, w_uvqk, w_out, cotangent)
    arrived = exchange(pieces)
    grad_t, squares = add_rows(asked, arrived, parity)
    squares = lax.all_to_all(squares, "col", split_axis=0, concat_axis=0, tiled=True)
    new_table_t, new_state = update(
        squares, ada_state.reshape(TOUCH // 128, 128), table_t, grad_t
    )
    return (layer_out, new_table_t.T, new_state.reshape(TOUCH))


def solution(mesh):
    in_specs = (
        P("table", "col"),
        P("table"),
        P(),
        P(),
        P("table", None, None),
        P("table", None),
        P(("table", "col"), None),
        P(("table", "col"), None),
    )
    out_specs = (P(("table", "col"), None), P("table", "col"), P("table"))
    return jax.shard_map(shards, mesh=mesh, in_specs=in_specs, out_specs=out_specs, check_vma=False)
```

time: 276 us -> 123 us (0.45)
  matrix products: 109 us -> 0 us
  blocking collectives: 13.2 us -> 78.5 us
  waiting for transfers between devices: 60.4 us -> 0 us
  local copies, waits for them, and re-layouts: 55.2 us -> 2.52 us
  Pallas kernels: 0 us -> 41.2 us
  starting transfers between devices: 23.1 us -> 0 us
  other arithmetic: 11.6 us -> 0 us
    dot_general x45 -> x0, matrix products: 109 us -> none  [the longest x16 35.1 us: add_one_block(): lax.dot_general(onehot, block_rows, (((0,), (0,)), ((), ())), preferred_e...]
    all_to_all x0 -> x4, blocking collectives: none -> 78.5 us  [the longest x2 56.2 us: exchange(): lax.all_to_all(blocks, ('table', 'col'), split_axis=0, concat_axis=0, til...]
    all_to_all x3 -> x0, waiting for transfers between devices: 60.4 us -> none  [the longest x1 27.8 us: shards(): lax.all_to_all(reply, ('table', 'col'), split_axis=0, concat_axis=0, tile...]
    pallas_call x0 -> x5, Pallas kernels: none -> 41.2 us  [the longest x1 24 us: layer(): pl.pallas_call(functools.partial(layer_kernel, member), out_shape=(jax.Sh...]
    reshape x10 -> x0, local copies, waits for them, and re-layouts: 27.1 us -> none  [the longest x2 7.4 us: pick_rows(): return picked.reshape(indices.shape + (source.shape[1],))]
    all_to_all x3 -> x0, starting transfers between devices: 23.1 us -> none  [the longest x1 11.5 us: shards(): lax.all_to_all(spread_ask.reshape(table_count * col_count, capacity), ('t...]
    psum x1 -> x0, blocking collectives: 13.2 us -> none  [shards(): squares = lax.psum(jnp.sum(row_grad * row_grad, axis=1), 'col')]
    unnamed x44 -> x18, local copies, waits for them, and re-layouts: 12.2 us -> 2.52 us
  transfers between devices with their start and end apart: 3 -> 0, of which waited for: 3 -> 0; matrix products, arithmetic and copies ran while one was open for 3% -> 0% of each run, Pallas kernels for 0% -> 0%
where the time goes in v1:
time: 123 us
  blocking collectives  78.5 us (64%)
  Pallas kernels  41.2 us (33%)
  local copies, waits for them, and re-layouts  2.52 us (2%)
    all_to_all x2, blocking collectives, exchange(): lax.all_to_all(blocks, ('table', 'col'), split_axis=0, concat_axis=0, til...  56.2 us
    pallas_call x1, Pallas kernels, layer(): pl.pallas_call(functools.partial(layer_kernel, member), out_shape=(jax.Sh...  24 us
    all_to_all x1, blocking collectives, shards(): lax.all_to_all(asks, 'table', split_axis=0, concat_axis=0, tiled=True)  13.9 us
    all_to_all x1, blocking collectives, shards(): lax.all_to_all(squares, 'col', split_axis=0, concat_axis=0, tiled=True)  8.45 us
    pallas_call x1, Pallas kernels, pick_rows(): pl.pallas_call(functools.partial(pick_kernel, parity), out_shape=jax.Shap...  8.16 us
    pallas_call x1, Pallas kernels, add_rows(): pl.pallas_call(functools.partial(add_kernel, parity), out_shape=(jax.Shap...  7.18 us
    unnamed x18, local copies, waits for them, and re-layouts  2.52 us

profile of v1, /device:TPU:1, one launch (start us, length us, event | category | flops | bytes accessed | tf_op | source)
XLA Modules:
  0.0 122.9 jit_solution(16871890984698561926)
XLA Ops:
  0.6 0.0 copy-start.5
  0.6 0.7 copy-done.5
  1.4 0.0 copy-start.6
  1.4 0.7 copy-done.6
  2.1 1.0 ask.1
  3.1 13.9 %all_to_all.20.asks_ref = s32[16,1,768]{2,1,0:T(1,128)S(1)} all-to-all(s32[16,1,768]{2,1,0:T(1,128)S(1)} %get-tuple-element.11), channel_id=1, replica_groups=mesh['table'=16,'col'=8] {'table'}, dimensions={0} | all-to-all | bytes 98304 | tf_op jit(solution)/shard_map/all_to_all | solution.py:410
  16.9 0.0 copy-start.1
  16.9 1.0 copy-done.1
  18.0 0.0 copy-start.3
  18.0 8.2 %pick.1 = bf16[16,320,128]{2,1,0:T(8,128)(2,1)S(1)} custom-call(s32[16,1,768]{2,1,0:T(1,128)S(1)} %all_to_all.20.asks_ref, f32[64,2048]{1,0:T(8,128)S(1)} %bitcast.12), custom_call_target="tpu_custom_call" | custom-call | tf_op jit(solution)/shard_map/pick/pallas_call | solution.py:127
  26.1 0.0 copy-start
  26.1 0.0 copy-start.4
  26.1 0.0 copy-start.8
  26.2 30.1 %all_to_all.21 = bf16[128,40,128]{2,1,0:T(8,128)(2,1)S(1)} all-to-all(bf16[128,40,128]{2,1,0:T(8,128)(2,1)S(1)} %bitcast.11), channel_id=1, replica_groups=mesh['table'=16,'col'=8] {'table','col'}, dimensions={0} | all-to-all | bytes 2621440 | tf_op jit(solution)/shard_map/all_to_all | solution.py:397
  56.2 0.0 copy-done.3
  56.2 0.0 copy-done
  56.2 0.0 copy-done.4
  56.3 0.0 copy-done.8
  56.3 24.0 %layer.1 = (bf16[640,512]{1,0:T(8,128)(2,1)}, bf16[16,320,128]{2,1,0:T(8,128)(2,1)S(1)}) custom-call(bf16[16,320,128]{2,1,0:T(8,128)(2,1)S(1)} %bitcast.9, s32[8,640]{1,0:T(8,128)S(1)} %get-tuple-element.12.place_ref, s32[1,640]{1,0:T(1,128)S(1)} %copy-done.8, bf16[512,2048]{1,0:T(8,128)(2,1)S(1)} %copy-done, bf16[512,512]{1,0:T(8,128)(2,1)S(1)} %copy-done.4, ...), custom_call_target="tpu_custom_call" | custom-call | tf_op jit(solution)/shard_map/layer/pallas_call | solution.py:367
  80.3 26.1 %all_to_all.22 = bf16[128,40,128]{2,1,0:T(8,128)(2,1)S(1)} all-to-all(bf16[128,40,128]{2,1,0:T(8,128)(2,1)S(1)} %bitcast.14), channel_id=1, replica_groups=mesh['table'=16,'col'=8] {'table','col'}, dimensions={0} | all-to-all | bytes 2621440 | tf_op jit(solution)/shard_map/all_to_all | solution.py:397
  106.4 0.0 copy-start.2
  106.4 0.0 copy-start.7
  106.4 7.2 %add.1 = (f32[64,2048]{1,0:T(8,128)S(1)}, f32[8,16,128]{2,1,0:T(8,128)S(1)}) custom-call(s32[16,1,768]{2,1,0:T(1,128)S(1)} %all_to_all.20.asks_ref, bf16[16,320,128]{2,1,0:T(8,128)(2,1)S(1)} %bitcast.10), custom_call_target="tpu_custom_call" | custom-call | tf_op jit(solution)/shard_map/add/pallas_call | solution.py:168
  113.6 8.5 %all_to_all.23.squares_ref = f32[8,16,128]{2,1,0:T(8,128)S(1)} all-to-all(f32[8,16,128]{2,1,0:T(8,128)S(1)} %get-tuple-element.15), channel_id=1, replica_groups=mesh['table'=16,'col'=8] {'col'}, dimensions={0} | all-to-all | bytes 131072 | tf_op jit(solution)/shard_map/all_to_all | solution.py:415
  122.0 0.0 copy-done.2
  122.1 0.0 copy-done.7
  122.1 0.9 update.1
Async XLA Ops:
  0.6 0.7 copy-start.5
  1.4 0.7 copy-start.6
  16.9 1.0 copy-start.1
  18.0 38.3 %copy-start.3 = (bf16[640,512]{1,0:T(8,128)(2,1)S(1)}, bf16[640,512]{1,0:T(8,128)(2,1)}, u32[]{:S(2)}) copy-start(bf16[640,512]{1,0:T(8,128)(2,1)} %cotangent_ref.1) | copy-start | bytes 1966084
  26.1 30.1 %copy-start = (bf16[512,2048]{1,0:T(8,128)(2,1)S(1)}, bf16[512,2048]{1,0:T(8,128)(2,1)}, u32[]{:S(2)}) copy-start(bf16[512,2048]{1,0:T(8,128)(2,1)} %w_ref.1) | copy-start | bytes 6291460
  26.1 30.1 %copy-start.4 = (bf16[512,512]{1,0:T(8,128)(2,1)S(1)}, bf16[512,512]{1,0:T(8,128)(2,1)}, u32[]{:S(2)}) copy-start(bf16[512,512]{1,0:T(8,128)(2,1)} %w_out_ref.1) | copy-start | bytes 1572868
  26.1 30.1 %copy-start.8 = (s32[1,640]{1,0:T(1,128)S(1)}, s32[1,640]{1,0:T(1,128)}, u32[]{:S(2)}) copy-start(s32[1,640]{1,0:T(1,128)} %segment_ref.1) | copy-start | bytes 7684
  106.4 15.6 %copy-start.2 = (f32[2048,64]{0,1:T(8,128)S(1)}, f32[2048,64]{0,1:T(8,128)}, u32[]{:S(2)}) copy-start(f32[2048,64]{0,1:T(8,128)} %param.8) | copy-start | bytes 1572868
  106.4 15.6 %copy-start.7 = (f32[2048]{0:T(1024)S(1)}, f32[2048]{0:T(1024)}, u32[]{:S(2)}) copy-start(f32[2048]{0:T(1024)} %param.9) | copy-start | bytes 24580

commit v2 on v1

v2 whole, which is shorter than its diff:
```python
import functools

import jax
import jax.numpy as jnp
from jax import lax
from jax.experimental import pallas as pl
from jax.experimental.pallas import tpu as pltpu
from jax.sharding import PartitionSpec as P

D = 512
HEADS = 4
HDIM = 128
TOK_DEV = 640
TABLES = 16
COLS = 8
CAP = 80
HALF = CAP // 2
TOUCH = 2048
WIDTH = D // COLS
HI = 256
HI_BITS = 8
LO = TOUCH // HI
ASKS = 768
BLOCK = 128
REACH = 288
REACH_TILES = 384
FAR = -1.0e4

NORM_EPS = 1e-05
ROOT_EPS = 1e-08
STEP_SIZE = 0.3

F32 = jnp.float32
BF16 = jnp.bfloat16
I32 = jnp.int32


def iota(shape, dim):
    return lax.broadcasted_iota(I32, shape, dim)


def nt_dot(a, b):
    return lax.dot_general(a, b, (((1,), (1,)), ((), ())), preferred_element_type=F32)


def tn_dot(a, b):
    return lax.dot_general(a, b, (((0,), (0,)), ((), ())), preferred_element_type=F32)


def params(megabytes):
    return pltpu.CompilerParams(vmem_limit_bytes=megabytes * 1024 * 1024)


def ask_kernel(owner_ref, slot_ref, asks_ref, place_ref):
    lower = jnp.where(iota((TOK_DEV, TOK_DEV), 0) <= iota((TOK_DEV, TOK_DEV), 1), 1.0, 0.0).astype(BF16)
    table = iota((TABLES, TOK_DEV), 0)
    spans = [slice(TOK_DEV * m, TOK_DEV * (m + 1)) for m in range(COLS)]
    hits = [jnp.where(owner_ref[:, span] == table, 1.0, 0.0) for span in spans]
    running = jnp.dot(
        jnp.concatenate(hits, axis=0).astype(BF16), lower, preferred_element_type=F32
    )
    lane = iota((TABLES, 128), 1)
    slot_at = iota((128, TOK_DEV), 0)
    tiles = [jnp.zeros((TABLES, 128), F32) for _ in range(ASKS // 128)]
    for m, span in enumerate(spans):
        count = running[TABLES * m : TABLES * (m + 1)] * hits[m]
        placing = jnp.sum(count, axis=0, keepdims=True).astype(I32) - 1
        onehot = jnp.where(slot_at == placing, 1.0, 0.0).astype(BF16)
        slot = slot_ref[:, span]
        high = (slot >> HI_BITS).astype(F32) * hits[m]
        low = (slot & (HI - 1)).astype(F32) * hits[m]
        found = nt_dot(jnp.concatenate([high, low], axis=0).astype(BF16), onehot)
        value = found[:TABLES] * float(HI) + found[TABLES:]
        for h in range(2):
            begin = h * (ASKS // 2) + m * HALF
            moved = pltpu.roll(value, (begin - h * HALF) % 128, 1)
            for j in range(begin // 128, (begin + HALF - 1) // 128 + 1):
                at = lane + 128 * j
                tiles[j] = jnp.where((at >= begin) & (at < begin + HALF), moved, tiles[j])
        place_ref[m : m + 1, :] = (
            owner_ref[:, span] * HALF
            + placing
            + jnp.where(placing >= HALF, TABLES * HALF - HALF, 0)
        )
    for j, tile in enumerate(tiles):
        asks_ref[:, 0, 128 * j : 128 * (j + 1)] = tile.astype(I32)


def make_asks(owner, slot):
    return pl.pallas_call(
        ask_kernel,
        out_shape=(
            jax.ShapeDtypeStruct((TABLES, 1, ASKS), I32),
            jax.ShapeDtypeStruct((COLS, TOK_DEV), I32),
        ),
        compiler_params=params(32),
        name="ask",
    )(owner, slot)


def ask_onehot(ask):
    rows = iota((HI, ASKS), 0).astype(F32).astype(BF16)
    wanted = (ask & (HI - 1)).astype(F32).astype(BF16)
    return jnp.where(rows == wanted, jnp.ones((), BF16), jnp.zeros((), BF16))


def rows_kernel(table_ref, rows_ref):
    for lo in range(LO):
        rows_ref[WIDTH * lo : WIDTH * (lo + 1), :] = table_ref[:, HI * lo : HI * (lo + 1)].astype(BF16)


def make_rows(table_t):
    return pl.pallas_call(
        rows_kernel,
        out_shape=jax.ShapeDtypeStruct((LO * WIDTH, HI), BF16),
        compiler_params=params(8),
        name="rows",
    )(table_t)


def pick_kernel(parity, asks_ref, rows_ref, reply_ref):
    par = parity()

    def one_group(g, carry):
        ask = asks_ref[g]
        found = jnp.dot(rows_ref[...], ask_onehot(ask), preferred_element_type=F32)
        low = jnp.broadcast_to(ask >> HI_BITS, (WIDTH, ASKS))
        parts = [found[WIDTH * lo : WIDTH * (lo + 1)] for lo in range(LO)]
        for bit in (1, 2, 4):
            upper = (low & bit) != 0
            parts = [jnp.where(upper, parts[i + 1], parts[i]) for i in range(0, len(parts), 2)]
        kept = parts[0]
        first, second = kept[:, : ASKS // 2], kept[:, ASKS // 2 :]
        stacked = jnp.concatenate(
            [jnp.where(par == 0, first, second), jnp.where(par == 0, second, first)], axis=0
        )
        reply_ref[g] = stacked.T[: COLS * HALF].astype(BF16)
        return carry

    lax.fori_loop(0, TABLES, one_group, 0, unroll=8)


def pick_rows(asks, rows, parity):
    return pl.pallas_call(
        functools.partial(pick_kernel, parity),
        out_shape=jax.ShapeDtypeStruct((TABLES, COLS * HALF, 128), BF16),
        compiler_params=params(32),
        name="pick",
    )(asks, rows)


def add_kernel(parity, asks_ref, arrived_ref, grad_ref, squares_ref, total_ref):
    par = parity()
    total_ref[...] = jnp.zeros_like(total_ref)
    empty = jnp.zeros((ASKS // 2 - COLS * HALF, 128), F32)

    def one_group(g, carry):
        ask = asks_ref[g]
        block = jnp.concatenate([arrived_ref[g].astype(F32), empty], axis=0).T
        upper, lower = block[:WIDTH], block[WIDTH:]
        slots = jnp.concatenate(
            [jnp.where(par == 0, upper, lower), jnp.where(par == 0, lower, upper)], axis=1
        )
        low = jnp.broadcast_to(ask >> HI_BITS, (WIDTH, ASKS))
        spread = jnp.concatenate(
            [jnp.where(low == lo, slots, 0.0).astype(BF16) for lo in range(LO)], axis=0
        )
        total_ref[...] += nt_dot(spread, ask_onehot(ask))
        return carry

    lax.fori_loop(0, TABLES, one_group, 0, unroll=16)
    sums = []
    for lo in range(LO):
        part = total_ref[WIDTH * lo : WIDTH * (lo + 1), :]
        grad_ref[:, HI * lo : HI * (lo + 1)] = part
        square = jnp.sum(part * part, axis=0, keepdims=True)
        sums += [square[:, :128], square[:, 128:]]
    squares = jnp.concatenate(sums, axis=0)
    for c in range(COLS):
        squares_ref[c] = squares


def add_rows(asks, arrived, parity):
    return pl.pallas_call(
        functools.partial(add_kernel, parity),
        out_shape=(
            jax.ShapeDtypeStruct((WIDTH, TOUCH), F32),
            jax.ShapeDtypeStruct((COLS, TOUCH // 128, 128), F32),
        ),
        scratch_shapes=[pltpu.VMEM((LO * WIDTH, HI), F32)],
        compiler_params=params(48),
        name="add",
    )(asks, arrived)


def update_kernel(squares_ref, state_ref, table_ref, grad_ref, new_table_ref, new_state_ref):
    squares = squares_ref[0]
    for c in range(1, COLS):
        squares = squares + squares_ref[c]
    state = state_ref[...] + squares / D
    new_state_ref[...] = state
    factor = STEP_SIZE / (jnp.sqrt(state) + ROOT_EPS)
    for i in range(TOUCH // 128):
        at = slice(128 * i, 128 * (i + 1))
        new_table_ref[:, at] = table_ref[:, at] - grad_ref[:, at] * factor[i : i + 1]


def update(squares, state, table_t, grad_t):
    return pl.pallas_call(
        update_kernel,
        out_shape=(
            jax.ShapeDtypeStruct((WIDTH, TOUCH), F32),
            jax.ShapeDtypeStruct((TOUCH // 128, 128), F32),
        ),
        compiler_params=params(16),
        name="update",
    )(squares, state, table_t, grad_t)


def normalise(values):
    center = values - jnp.mean(values, axis=-1, keepdims=True)
    root = lax.rsqrt(jnp.mean(center * center, axis=-1, keepdims=True) + NORM_EPS)
    return center * root, root


def normalise_back(grad, normed, root):
    along = jnp.mean(grad * normed, axis=-1, keepdims=True)
    return root * (grad - jnp.mean(grad, axis=-1, keepdims=True) - normed * along)


def columns_of(row):
    return jnp.broadcast_to(row.astype(F32), (128, TOK_DEV)).T


def layer_kernel(
    member,
    received_ref,
    place_ref,
    segment_ref,
    w_ref,
    w_out_ref,
    cotangent_ref,
    out_ref,
    pieces_ref,
    slots_ref,
    segment_col,
    embedded_ref,
    normed_ref,
    gates_ref,
    slope_ref,
    values_ref,
    queries_ref,
    keys_ref,
    weights_ref,
    score_slope_ref,
    attended_ref,
    grad_attended_ref,
    grad_queries_ref,
    grad_u_ref,
    token_grad_ref,
):
    place = place_ref[pl.ds(member(), 1), :]
    segment_col[...] = columns_of(segment_ref[...])
    left = iota((HALF, 128), 1) < WIDTH
    four = 4 * HALF
    units = [
        (j, h, slice(BLOCK * j, min(TOK_DEV, BLOCK * j + REACH)), slice(BLOCK * j, BLOCK * (j + 1)), slice(HDIM * h, HDIM * (h + 1)))
        for j in range(TOK_DEV // BLOCK)
        for h in range(HEADS)
    ]

    def gather_slots(t, carry):
        parts = []
        for i in range(4):
            block = received_ref[4 * t + i].astype(F32)
            parts.append([block[HALF * c : HALF * (c + 1)] for c in range(COLS)])
        at = pl.multiple_of(four * t, four)
        for j in range(COLS // 2):
            pairs = [(part[2 * j], part[2 * j + 1]) for part in parts]
            first = [jnp.where(left, even, odd) for even, odd in pairs]
            second = [pltpu.roll(jnp.where(left, odd, even), WIDTH, 1) for even, odd in pairs]
            tile = slice(128 * j, 128 * (j + 1))
            slots_ref[pl.ds(at, four), tile] = jnp.concatenate(first, axis=0).astype(BF16)
            slots_ref[pl.ds(TABLES * HALF + at, four), tile] = jnp.concatenate(second, axis=0).astype(BF16)
        return carry

    lax.fori_loop(0, TABLES // 4, gather_slots, 0)

    at = columns_of(place).astype(I32)
    lane = iota((TOK_DEV, 128), 1)
    onehot = jnp.concatenate(
        [jnp.where(at == lane + 128 * j, 1.0, 0.0).astype(BF16) for j in range(TABLES * CAP // 128)],
        axis=1,
    )
    embedded = jnp.dot(onehot, slots_ref[...], preferred_element_type=F32)
    embedded_ref[...] = embedded.astype(BF16)
    normed, root = normalise(embedded)
    normed_ref[...] = normed.astype(BF16)
    piece = 256
    for p in range(4 * D // piece):
        part = slice(piece * p, piece * (p + 1))
        linear = 0.5 * jnp.dot(normed_ref[...], w_ref[:, part], preferred_element_type=F32)
        bend = jnp.tanh(linear)
        swish = linear + linear * bend
        gate = 0.5 + 0.5 * bend
        ref = (gates_ref, values_ref, queries_ref, keys_ref)[piece * p // D]
        within = piece * p % D
        ref[:, within : within + piece] = swish.astype(ref.dtype)
        slope_ref[:, part] = gate + swish * (1.0 - gate)

    scale = HDIM**-0.5
    attended_ref[...] = jnp.zeros_like(attended_ref)
    for j, h, rows, keys, head in units:
        length = rows.stop - rows.start
        allowed = segment_col[rows, :] == segment_ref[:, keys].astype(F32)
        allowed = allowed & (iota((length, BLOCK), 0) >= iota((length, BLOCK), 1))
        scores = nt_dot(queries_ref[rows, head], keys_ref[keys, head])
        scores = jnp.where(allowed, scores * (0.5 * scale), FAR)
        bend = jnp.tanh(scores)
        swish = scores + scores * bend
        gate = 0.5 + 0.5 * bend
        weights = swish.astype(BF16)
        weights_ref[HEADS * j + h, :, :length] = weights.T
        score_slope_ref[HEADS * j + h, :length, :] = scale * (gate + swish * (1.0 - gate))
        attended_ref[rows, head] += jnp.dot(weights, values_ref[keys, head], preferred_element_type=F32)

    again, root_again = normalise(attended_ref[...])
    gated = (again * gates_ref[...]).astype(BF16)
    out = jnp.dot(gated, w_out_ref[...], preferred_element_type=F32)
    out_ref[...] = (out + embedded_ref[...].astype(F32)).astype(BF16)
    grad_gated = nt_dot(cotangent_ref[...], w_out_ref[...]).astype(BF16).astype(F32)
    grad_u_ref[:, :D] = (grad_gated * again * slope_ref[:, :D]).astype(BF16)
    grad_attended_ref[...] = normalise_back(grad_gated * gates_ref[...], again, root_again).astype(BF16)

    grad_queries_ref[...] = jnp.zeros_like(grad_queries_ref)
    for j, h, rows, keys, head in units:
        length = rows.stop - rows.start
        grad_weights = nt_dot(grad_attended_ref[rows, head], values_ref[keys, head])
        grad_scores = (grad_weights * score_slope_ref[HEADS * j + h, :length, :]).astype(BF16)
        grad_queries_ref[rows, head] += jnp.dot(grad_scores, keys_ref[keys, head], preferred_element_type=F32)
        grad_values = jnp.dot(
            weights_ref[HEADS * j + h, :, :length], grad_attended_ref[rows, head], preferred_element_type=F32
        )
        grad_keys = tn_dot(grad_scores, queries_ref[rows, head])
        for k, grad in ((1, grad_values), (3, grad_keys)):
            part = slice(k * D + head.start, k * D + head.stop)
            grad_u_ref[keys, part] = (grad * slope_ref[keys, part]).astype(BF16)
    grad_u_ref[:, 2 * D : 3 * D] = (grad_queries_ref[...] * slope_ref[:, 2 * D : 3 * D]).astype(BF16)

    grad = nt_dot(grad_u_ref[...], w_ref[...])
    grad = normalise_back(grad, normed_ref[...].astype(F32), root)
    token_grad_ref[...] = (grad + cotangent_ref[...].astype(F32)).astype(BF16)

    onehot = jnp.where(place == iota((TABLES * CAP, TOK_DEV), 0), 1.0, 0.0).astype(BF16)
    half = TABLES * HALF
    for j in range(COLS // 2):
        if j % 2 == 0:
            part = slice(128 * j, 128 * (j + 2))
            sent = jnp.dot(onehot, token_grad_ref[:, part], preferred_element_type=F32)
        tile = slice(128 * (j % 2), 128 * (j % 2 + 1))
        first, second = sent[:half, tile], pltpu.roll(sent[half:, tile], WIDTH, 1)
        wide = iota((half, 128), 1) < WIDTH
        even, odd = jnp.where(wide, first, second), jnp.where(wide, second, first)
        for t in range(TABLES):
            rows = slice(HALF * t, HALF * (t + 1))
            pieces_ref[t, 2 * HALF * j : 2 * HALF * (j + 1), :] = jnp.concatenate(
                [even[rows], odd[rows]], axis=0
            ).astype(BF16)


def layer(received, place, member, segment, w_uvqk, w_out, cotangent):
    count = TOK_DEV // BLOCK * HEADS
    return pl.pallas_call(
        functools.partial(layer_kernel, member),
        out_shape=(
            jax.ShapeDtypeStruct((TOK_DEV, D), BF16),
            jax.ShapeDtypeStruct((TABLES, COLS * HALF, 128), BF16),
        ),
        scratch_shapes=[
            pltpu.VMEM((TABLES * CAP, D), BF16),
            pltpu.VMEM((TOK_DEV, 128), F32),
            pltpu.VMEM((TOK_DEV, D), BF16),
            pltpu.VMEM((TOK_DEV, D), BF16),
            pltpu.VMEM((TOK_DEV, D), F32),
            pltpu.VMEM((TOK_DEV, 4 * D), F32),
            pltpu.VMEM((TOK_DEV, D), BF16),
            pltpu.VMEM((TOK_DEV, D), BF16),
            pltpu.VMEM((TOK_DEV, D), BF16),
            pltpu.VMEM((count, BLOCK, REACH_TILES), BF16),
            pltpu.VMEM((count, REACH, BLOCK), F32),
            pltpu.VMEM((TOK_DEV, D), F32),
            pltpu.VMEM((TOK_DEV, D), BF16),
            pltpu.VMEM((TOK_DEV, D), F32),
            pltpu.VMEM((TOK_DEV, 4 * D), BF16),
            pltpu.VMEM((TOK_DEV, D), BF16),
        ],
        compiler_params=params(48),
        name="layer",
    )(received, place, segment, w_uvqk, w_out, cotangent)


def exchange(blocks):
    blocks = blocks.reshape(TABLES * COLS, HALF, 128)
    blocks = lax.all_to_all(blocks, ("table", "col"), split_axis=0, concat_axis=0, tiled=True)
    return blocks.reshape(TABLES, COLS * HALF, 128)


def shards(table_rows, ada_state, w_uvqk, w_out, tok_owner, tok_slot, seg_ids, cotangent):
    def member():
        return lax.axis_index("col")

    def parity():
        return lax.axis_index("col") % 2

    table_t = table_rows.T
    asks, place = make_asks(tok_owner.reshape(1, COLS * TOK_DEV), tok_slot)
    asked = lax.all_to_all(asks, "table", split_axis=0, concat_axis=0, tiled=True)
    received = exchange(pick_rows(asked, make_rows(table_t), parity))
    layer_out, pieces = layer(received, place, member, seg_ids, w_uvqk, w_out, cotangent)
    arrived = exchange(pieces)
    grad_t, squares = add_rows(asked, arrived, parity)
    squares = lax.all_to_all(squares, "col", split_axis=0, concat_axis=0, tiled=True)
    new_table_t, new_state = update(
        squares, ada_state.reshape(TOUCH // 128, 128), table_t, grad_t
    )
    return (layer_out, new_table_t.T, new_state.reshape(TOUCH))


def solution(mesh):
    in_specs = (
        P("table", "col"),
        P("table"),
        P(),
        P(),
        P("table", None, None),
        P("table", None),
        P(("table", "col"), None),
        P(("table", "col"), None),
    )
    out_specs = (P(("table", "col"), None), P("table", "col"), P("table"))
    return jax.shard_map(shards, mesh=mesh, in_specs=in_specs, out_specs=out_specs, check_vma=False)
```

time: 123 us -> 106 us (0.86)
  Pallas kernels: 41.2 us -> 24.3 us
  blocking collectives: 78.5 us -> 64.6 us
  starting transfers between devices: 0 us -> 7.58 us
  waiting for transfers between devices: 0 us -> 5.41 us
    all_to_all x1 -> x0, blocking collectives: 13.9 us -> none  [shards(): lax.all_to_all(asks, 'table', split_axis=0, concat_axis=0, tiled=True)]
    pallas_call x1, Pallas kernels: 24 us -> 14.3 us  [layer(): pl.pallas_call(functools.partial(layer_kernel, member), out_shape=(jax.Sh...]
    all_to_all x0 -> x1, starting transfers between devices: none -> 7.58 us  [shards(): lax.all_to_all(asks, 'table', split_axis=0, concat_axis=0, tiled=True)]
    all_to_all x0 -> x1, waiting for transfers between devices: none -> 5.41 us  [shards(): lax.all_to_all(asks, 'table', split_axis=0, concat_axis=0, tiled=True)]
    pallas_call x1, Pallas kernels: 8.16 us -> 4.06 us  [pick_rows(): pl.pallas_call(functools.partial(pick_kernel, parity), out_shape=jax.Shap...]
    pallas_call x1, Pallas kernels: 7.18 us -> 3.5 us  [add_rows(): pl.pallas_call(functools.partial(add_kernel, parity), out_shape=(jax.Shap...]
  transfers between devices with their start and end apart: 0 -> 1, of which waited for: 0 -> 1; matrix products, arithmetic and copies ran while one was open for 0% -> 0% of each run, Pallas kernels for 0% -> 0%
where the time goes in v2:
time: 106 us; the launch traced here: 105 us
  blocking collectives  64.6 us (61%)
  Pallas kernels  24.3 us (23%)
  starting transfers between devices  7.58 us (7%)
  waiting for transfers between devices  5.41 us (5%)
  local copies, waits for them, and re-layouts  2.51 us (2%)
    all_to_all x2, blocking collectives, exchange(): lax.all_to_all(blocks, ('table', 'col'), split_axis=0, concat_axis=0, til...  56.2 us
    pallas_call x1, Pallas kernels, layer(): pl.pallas_call(functools.partial(layer_kernel, member), out_shape=(jax.Sh...  14.3 us
    all_to_all x1, blocking collectives, shards(): lax.all_to_all(squares, 'col', split_axis=0, concat_axis=0, tiled=True)  8.45 us
    all_to_all x1, starting transfers between devices, shards(): lax.all_to_all(asks, 'table', split_axis=0, concat_axis=0, tiled=True)  7.58 us
    all_to_all x1, waiting for transfers between devices, shards(): lax.all_to_all(asks, 'table', split_axis=0, concat_axis=0, tiled=True)  5.41 us
    pallas_call x1, Pallas kernels, pick_rows(): pl.pallas_call(functools.partial(pick_kernel, parity), out_shape=jax.Shap...  4.06 us
    pallas_call x1, Pallas kernels, add_rows(): pl.pallas_call(functools.partial(add_kernel, parity), out_shape=(jax.Shap...  3.5 us
    unnamed x18, local copies, waits for them, and re-layouts  2.51 us
  transfers between devices with their start and end apart: 1, of which 1 were waited for; matrix products, arithmetic and copies ran while one was open for 0% of the time, Pallas kernels for 0%

profile of v2, /device:TPU:1, one launch (start us, length us, event | category | flops | bytes accessed | tf_op | source)
XLA Modules:
  0.0 105.2 jit_solution(10241421722934507813)
XLA Ops:
  0.6 0.0 copy-start.5
  0.6 0.7 copy-done.5
  1.4 0.0 copy-start.6
  1.4 0.7 copy-done.6
  2.1 1.6 %ask.1 = (s32[16,1,768]{2,1,0:T(1,128)}, s32[8,640]{1,0:T(8,128)S(1)}) custom-call(s32[1,5120]{1,0:T(1,128)S(1)} %bitcast.15, s32[1,5120]{1,0:T(1,128)S(1)} %copy-done.6), custom_call_target="tpu_custom_call" | custom-call | tf_op jit(solution)/shard_map/ask/pallas_call | solution.py:90
  3.7 7.6 %all-to-all-start = ((s32[16,1,768]{2,1,0:T(1,128)}), s32[16,1,768]{2,1,0:T(1,128)S(1)}, u32[]{:S(2)}, u32[]{:S(2)}) async-start(s32[16,1,768]{2,1,0:T(1,128)} %get-tuple-element.11), calls=%async_computation | async-start | bytes 98304 | tf_op jit(solution)/shard_map/all_to_all | solution.py:417
  11.3 0.0 copy-start.1
  11.3 1.0 copy-done.1
  12.3 5.4 %all-to-all-done.asks_ref = s32[16,1,768]{2,1,0:T(1,128)S(1)} async-done(((s32[16,1,768]{2,1,0:T(1,128)}), s32[16,1,768]{2,1,0:T(1,128)S(1)}, u32[]{:S(2)}, u32[]{:S(2)}) %all-to-all-start) | async-done | bytes 49184 | tf_op jit(solution)/shard_map/all_to_all | solution.py:417
  17.7 0.0 copy-start.3
  17.7 4.1 %pick.1 = bf16[16,320,128]{2,1,0:T(8,128)(2,1)S(1)} custom-call(s32[16,1,768]{2,1,0:T(1,128)S(1)} %all-to-all-done.asks_ref, bf16[512,256]{1,0:T(8,128)(2,1)S(1)} %rows.1.rows_ref), custom_call_target="tpu_custom_call" | custom-call | tf_op jit(solution)/shard_map/pick/pallas_call | solution.py:144
  21.8 0.0 copy-start
  21.8 0.0 copy-start.4
  21.8 0.0 copy-start.8
  21.8 30.1 %all_to_all.20 = bf16[128,40,128]{2,1,0:T(8,128)(2,1)S(1)} all-to-all(bf16[128,40,128]{2,1,0:T(8,128)(2,1)S(1)} %bitcast.11), channel_id=1, replica_groups=mesh['table'=16,'col'=8] {'table','col'}, dimensions={0} | all-to-all | bytes 2621440 | tf_op jit(solution)/shard_map/all_to_all | solution.py:404
  51.9 0.0 copy-done.3
  51.9 0.0 copy-done
  51.9 0.0 copy-done.4
  51.9 0.0 copy-done.8
  51.9 14.3 %layer.1 = (bf16[640,512]{1,0:T(8,128)(2,1)}, bf16[16,320,128]{2,1,0:T(8,128)(2,1)S(1)}) custom-call(bf16[16,320,128]{2,1,0:T(8,128)(2,1)S(1)} %bitcast.9, s32[8,640]{1,0:T(8,128)S(1)} %get-tuple-element.12.place_ref, s32[1,640]{1,0:T(1,128)S(1)} %copy-done.8, bf16[512,2048]{1,0:T(8,128)(2,1)S(1)} %copy-done, bf16[512,512]{1,0:T(8,128)(2,1)S(1)} %copy-done.4, ...), custom_call_target="tpu_custom_call" | custom-call | tf_op jit(solution)/shard_map/layer/pallas_call | solution.py:373
  66.2 26.1 %all_to_all.21 = bf16[128,40,128]{2,1,0:T(8,128)(2,1)S(1)} all-to-all(bf16[128,40,128]{2,1,0:T(8,128)(2,1)S(1)} %bitcast.14), channel_id=1, replica_groups=mesh['table'=16,'col'=8] {'table','col'}, dimensions={0} | all-to-all | bytes 2621440 | tf_op jit(solution)/shard_map/all_to_all | solution.py:404
  92.3 0.0 copy-start.2
  92.3 0.0 copy-start.7
  92.3 3.5 %add.1 = (f32[64,2048]{1,0:T(8,128)S(1)}, f32[8,16,128]{2,1,0:T(8,128)S(1)}) custom-call(s32[16,1,768]{2,1,0:T(1,128)S(1)} %all-to-all-done.asks_ref, bf16[16,320,128]{2,1,0:T(8,128)(2,1)S(1)} %bitcast.10), custom_call_target="tpu_custom_call" | custom-call | tf_op jit(solution)/shard_map/add/pallas_call | solution.py:184
  95.8 8.5 %all_to_all.22.squares_ref = f32[8,16,128]{2,1,0:T(8,128)S(1)} all-to-all(f32[8,16,128]{2,1,0:T(8,128)S(1)} %get-tuple-element.15), channel_id=1, replica_groups=mesh['table'=16,'col'=8] {'col'}, dimensions={0} | all-to-all | bytes 131072 | tf_op jit(solution)/shard_map/all_to_all | solution.py:422
  104.3 0.0 copy-done.2
  104.3 0.0 copy-done.7
  104.3 0.9 update.1
  (1 shorter events, 0.0 us)
Async XLA Ops:
  0.6 0.7 copy-start.5
  1.4 0.7 copy-start.6
  3.7 14.1 %all-to-all-start = ((s32[16,1,768]{2,1,0:T(1,128)}), s32[16,1,768]{2,1,0:T(1,128)S(1)}, u32[]{:S(2)}, u32[]{:S(2)}) async-start(s32[16,1,768]{2,1,0:T(1,128)} %get-tuple-element.11), calls=%async_computation | async-start | bytes 98304 | tf_op jit(solution)/shard_map/all_to_all | solution.py:417
  11.3 1.0 copy-start.1
  17.7 34.2 %copy-start.3 = (bf16[640,512]{1,0:T(8,128)(2,1)S(1)}, bf16[640,512]{1,0:T(8,128)(2,1)}, u32[]{:S(2)}) copy-start(bf16[640,512]{1,0:T(8,128)(2,1)} %cotangent_ref.1) | copy-start | bytes 1966084
  21.8 30.1 %copy-start = (bf16[512,2048]{1,0:T(8,128)(2,1)S(1)}, bf16[512,2048]{1,0:T(8,128)(2,1)}, u32[]{:S(2)}) copy-start(bf16[512,2048]{1,0:T(8,128)(2,1)} %w_ref.1) | copy-start | bytes 6291460
  21.8 30.1 %copy-start.4 = (bf16[512,512]{1,0:T(8,128)(2,1)S(1)}, bf16[512,512]{1,0:T(8,128)(2,1)}, u32[]{:S(2)}) copy-start(bf16[512,512]{1,0:T(8,128)(2,1)} %w_out_ref.1) | copy-start | bytes 1572868
  21.8 30.1 %copy-start.8 = (s32[1,640]{1,0:T(1,128)S(1)}, s32[1,640]{1,0:T(1,128)}, u32[]{:S(2)}) copy-start(s32[1,640]{1,0:T(1,128)} %segment_ref.1) | copy-start | bytes 7684
  92.3 12.0 %copy-start.2 = (f32[2048,64]{0,1:T(8,128)S(1)}, f32[2048,64]{0,1:T(8,128)}, u32[]{:S(2)}) copy-start(f32[2048,64]{0,1:T(8,128)} %param.8) | copy-start | bytes 1572868
  92.3 12.0 %copy-start.7 = (f32[2048]{0:T(1024)S(1)}, f32[2048]{0:T(1024)}, u32[]{:S(2)}) copy-start(f32[2048]{0:T(1024)} %param.9) | copy-start | bytes 24580

commit v3 on v2

--- a/solution.py
+++ b/solution.py
@@ -20,9 +20,11 @@
 HI = 256
 HI_BITS = 8
 LO = TOUCH // HI
-ASKS = 768
+ASKS = 640
 BLOCK = 128
 REACH = 288
+DEPTH = 2
+PAIR = 2 * ASKS
 REACH_TILES = 384
 FAR = -1.0e4
 
@@ -51,24 +53,31 @@
     return pltpu.CompilerParams(vmem_limit_bytes=megabytes * 1024 * 1024)
 
 
+def spans_of(row_ref):
+    return [row_ref[:, TOK_DEV * m : TOK_DEV * (m + 1)] for m in range(COLS)]
+
+
+def hits_of(owner_ref):
+    table = iota((TABLES, TOK_DEV), 0)
+    return [jnp.where(owner == table, 1.0, 0.0) for owner in spans_of(owner_ref)]
+
+
 def ask_kernel(owner_ref, slot_ref, asks_ref, place_ref):
     lower = jnp.where(iota((TOK_DEV, TOK_DEV), 0) <= iota((TOK_DEV, TOK_DEV), 1), 1.0, 0.0).astype(BF16)
-    table = iota((TABLES, TOK_DEV), 0)
-    spans = [slice(TOK_DEV * m, TOK_DEV * (m + 1)) for m in range(COLS)]
-    hits = [jnp.where(owner_ref[:, span] == table, 1.0, 0.0) for span in spans]
+    hits = hits_of(owner_ref)
     running = jnp.dot(
         jnp.concatenate(hits, axis=0).astype(BF16), lower, preferred_element_type=F32
     )
     lane = iota((TABLES, 128), 1)
     slot_at = iota((128, TOK_DEV), 0)
     tiles = [jnp.zeros((TABLES, 128), F32) for _ in range(ASKS // 128)]
-    for m, span in enumerate(spans):
-        count = running[TABLES * m : TABLES * (m + 1)] * hits[m]
+    members = zip(hits, spans_of(owner_ref), spans_of(slot_ref))
+    for m, (hit, owner, slot) in enumerate(members):
+        count = running[TABLES * m : TABLES * (m + 1)] * hit
         placing = jnp.sum(count, axis=0, keepdims=True).astype(I32) - 1
         onehot = jnp.where(slot_at == placing, 1.0, 0.0).astype(BF16)
-        slot = slot_ref[:, span]
-        high = (slot >> HI_BITS).astype(F32) * hits[m]
-        low = (slot & (HI - 1)).astype(F32) * hits[m]
+        high = (slot >> HI_BITS).astype(F32) * hit
+        low = (slot & (HI - 1)).astype(F32) * hit
         found = nt_dot(jnp.concatenate([high, low], axis=0).astype(BF16), onehot)
         value = found[:TABLES] * float(HI) + found[TABLES:]
         for h in range(2):
@@ -78,9 +87,7 @@
                 at = lane + 128 * j
                 tiles[j] = jnp.where((at >= begin) & (at < begin + HALF), moved, tiles[j])
         place_ref[m : m + 1, :] = (
-            owner_ref[:, span] * HALF
-            + placing
-            + jnp.where(placing >= HALF, TABLES * HALF - HALF, 0)
+            owner * HALF + placing + jnp.where(placing >= HALF, TABLES * HALF - HALF, 0)
         )
     for j, tile in enumerate(tiles):
         asks_ref[:, 0, 128 * j : 128 * (j + 1)] = tile.astype(I32)
@@ -93,13 +100,21 @@
             jax.ShapeDtypeStruct((TABLES, 1, ASKS), I32),
             jax.ShapeDtypeStruct((COLS, TOK_DEV), I32),
         ),
-        compiler_params=params(32),
+        compiler_params=params(16),
         name="ask",
     )(owner, slot)
 
 
+def ask_pair(asks_ref, i):
+    even, odd = asks_ref[2 * i], asks_ref[2 * i + 1]
+    first = iota((1, ASKS), 1) < ASKS // 2
+    low = jnp.where(first, even, pltpu.roll(odd, ASKS // 2, 1))
+    high = jnp.where(first, pltpu.roll(even, ASKS // 2, 1), odd)
+    return jnp.concatenate([low, high], axis=1)
+
+
 def ask_onehot(ask):
-    rows = iota((HI, ASKS), 0).astype(F32).astype(BF16)
+    rows = iota((HI, PAIR), 0).astype(F32).astype(BF16)
     wanted = (ask & (HI - 1)).astype(F32).astype(BF16)
     return jnp.where(rows == wanted, jnp.ones((), BF16), jnp.zeros((), BF16))
 
@@ -121,23 +136,25 @@
 def pick_kernel(parity, asks_ref, rows_ref, reply_ref):
     par = parity()
 
-    def one_group(g, carry):
-        ask = asks_ref[g]
+    def two_groups(i, carry):
+        ask = ask_pair(asks_ref, i)
         found = jnp.dot(rows_ref[...], ask_onehot(ask), preferred_element_type=F32)
-        low = jnp.broadcast_to(ask >> HI_BITS, (WIDTH, ASKS))
+        low = jnp.broadcast_to(ask >> HI_BITS, (WIDTH, PAIR))
         parts = [found[WIDTH * lo : WIDTH * (lo + 1)] for lo in range(LO)]
         for bit in (1, 2, 4):
             upper = (low & bit) != 0
             parts = [jnp.where(upper, parts[i + 1], parts[i]) for i in range(0, len(parts), 2)]
         kept = parts[0]
-        first, second = kept[:, : ASKS // 2], kept[:, ASKS // 2 :]
+        first, second = kept[:, :ASKS], kept[:, ASKS:]
         stacked = jnp.concatenate(
             [jnp.where(par == 0, first, second), jnp.where(par == 0, second, first)], axis=0
         )
-        reply_ref[g] = stacked.T[: COLS * HALF].astype(BF16)
+        replies = stacked.T.astype(BF16)
+        reply_ref[2 * i] = replies[: COLS * HALF]
+        reply_ref[2 * i + 1] = replies[COLS * HALF :]
         return carry
 
-    lax.fori_loop(0, TABLES, one_group, 0, unroll=8)
+    lax.fori_loop(0, TABLES // 2, two_groups, 0, unroll=8)
 
 
 def pick_rows(asks, rows, parity):
@@ -152,32 +169,29 @@
 def add_kernel(parity, asks_ref, arrived_ref, grad_ref, squares_ref, total_ref):
     par = parity()
     total_ref[...] = jnp.zeros_like(total_ref)
-    empty = jnp.zeros((ASKS // 2 - COLS * HALF, 128), F32)
-
-    def one_group(g, carry):
-        ask = asks_ref[g]
-        block = jnp.concatenate([arrived_ref[g].astype(F32), empty], axis=0).T
+
+    def two_groups(i, carry):
+        ask = ask_pair(asks_ref, i)
+        block = jnp.concatenate([arrived_ref[2 * i], arrived_ref[2 * i + 1]], axis=0).astype(F32).T
         upper, lower = block[:WIDTH], block[WIDTH:]
         slots = jnp.concatenate(
             [jnp.where(par == 0, upper, lower), jnp.where(par == 0, lower, upper)], axis=1
         )
-        low = jnp.broadcast_to(ask >> HI_BITS, (WIDTH, ASKS))
+        low = jnp.broadcast_to(ask >> HI_BITS, (WIDTH, PAIR))
         spread = jnp.concatenate(
             [jnp.where(low == lo, slots, 0.0).astype(BF16) for lo in range(LO)], axis=0
         )
         total_ref[...] += nt_dot(spread, ask_onehot(ask))
         return carry
 
-    lax.fori_loop(0, TABLES, one_group, 0, unroll=16)
+    lax.fori_loop(0, TABLES // 2, two_groups, 0, unroll=8)
     sums = []
     for lo in range(LO):
         part = total_ref[WIDTH * lo : WIDTH * (lo + 1), :]
         grad_ref[:, HI * lo : HI * (lo + 1)] = part
         square = jnp.sum(part * part, axis=0, keepdims=True)
         sums += [square[:, :128], square[:, 128:]]
-    squares = jnp.concatenate(sums, axis=0)
-    for c in range(COLS):
-        squares_ref[c] = squares
+    squares_ref[...] = jnp.concatenate(sums, axis=0)
 
 
 def add_rows(asks, arrived, parity):
@@ -185,7 +199,7 @@
         functools.partial(add_kernel, parity),
         out_shape=(
             jax.ShapeDtypeStruct((WIDTH, TOUCH), F32),
-            jax.ShapeDtypeStruct((COLS, TOUCH // 128, 128), F32),
+            jax.ShapeDtypeStruct((TOUCH // 128, 128), F32),
         ),
         scratch_shapes=[pltpu.VMEM((LO * WIDTH, HI), F32)],
         compiler_params=params(48),
@@ -193,10 +207,8 @@
     )(asks, arrived)
 
 
-def update_kernel(squares_ref, state_ref, table_ref, grad_ref, new_table_ref, new_state_ref):
-    squares = squares_ref[0]
-    for c in range(1, COLS):
-        squares = squares + squares_ref[c]
+def update_kernel(own_ref, near_ref, far_ref, last_ref, state_ref, table_ref, grad_ref, new_table_ref, new_state_ref):
+    squares = (own_ref[...] + near_ref[...]) + (far_ref[...] + last_ref[...])
     state = state_ref[...] + squares / D
     new_state_ref[...] = state
     factor = STEP_SIZE / (jnp.sqrt(state) + ROOT_EPS)
@@ -214,7 +226,7 @@
         ),
         compiler_params=params(16),
         name="update",
-    )(squares, state, table_t, grad_t)
+    )(*squares, state, table_t, grad_t)
 
 
 def normalise(values):
@@ -274,17 +286,18 @@
         for i in range(4):
             block = received_ref[4 * t + i].astype(F32)
             parts.append([block[HALF * c : HALF * (c + 1)] for c in range(COLS)])
-        at = pl.multiple_of(four * t, four)
+        at = four * t
         for j in range(COLS // 2):
             pairs = [(part[2 * j], part[2 * j + 1]) for part in parts]
             first = [jnp.where(left, even, odd) for even, odd in pairs]
             second = [pltpu.roll(jnp.where(left, odd, even), WIDTH, 1) for even, odd in pairs]
             tile = slice(128 * j, 128 * (j + 1))
-            slots_ref[pl.ds(at, four), tile] = jnp.concatenate(first, axis=0).astype(BF16)
-            slots_ref[pl.ds(TABLES * HALF + at, four), tile] = jnp.concatenate(second, axis=0).astype(BF16)
+            slots_ref[slice(at, at + four), tile] = jnp.concatenate(first, axis=0).astype(BF16)
+            slots_ref[slice(TABLES * HALF + at, TABLES * HALF + at + four), tile] = jnp.concatenate(second, axis=0).astype(BF16)
         return carry
 
-    lax.fori_loop(0, TABLES // 4, gather_slots, 0)
+    for t in range(TABLES // 4):
+        gather_slots(t, 0)
 
     at = columns_of(place).astype(I32)
     lane = iota((TOK_DEV, 128), 1)
@@ -297,9 +310,17 @@
     normed, root = normalise(embedded)
     normed_ref[...] = normed.astype(BF16)
     piece = 256
+    def project(p):
+        return jnp.dot(
+            normed_ref[...], w_ref[:, piece * p : piece * (p + 1)], preferred_element_type=F32
+        )
+
+    ahead = project(0)
     for p in range(4 * D // piece):
         part = slice(piece * p, piece * (p + 1))
-        linear = 0.5 * jnp.dot(normed_ref[...], w_ref[:, part], preferred_element_type=F32)
+        linear = 0.5 * ahead
+        if p + 1 < 4 * D // piece:
+            ahead = project(p + 1)
         bend = jnp.tanh(linear)
         swish = linear + linear * bend
         gate = 0.5 + 0.5 * bend
@@ -310,11 +331,18 @@
 
     scale = HDIM**-0.5
     attended_ref[...] = jnp.zeros_like(attended_ref)
-    for j, h, rows, keys, head in units:
+    def score(unit):
+        j, h, rows, keys, head = unit
+        return nt_dot(queries_ref[rows, head], keys_ref[keys, head])
+
+    ahead = [score(units[u]) for u in range(DEPTH)]
+    for u, (j, h, rows, keys, head) in enumerate(units):
         length = rows.stop - rows.start
         allowed = segment_col[rows, :] == segment_ref[:, keys].astype(F32)
         allowed = allowed & (iota((length, BLOCK), 0) >= iota((length, BLOCK), 1))
-        scores = nt_dot(queries_ref[rows, head], keys_ref[keys, head])
+        scores = ahead.pop(0)
+        if u + DEPTH < len(units):
+            ahead.append(score(units[u + DEPTH]))
         scores = jnp.where(allowed, scores * (0.5 * scale), FAR)
         bend = jnp.tanh(scores)
         swish = scores + scores * bend
@@ -333,9 +361,16 @@
     grad_attended_ref[...] = normalise_back(grad_gated * gates_ref[...], again, root_again).astype(BF16)
 
     grad_queries_ref[...] = jnp.zeros_like(grad_queries_ref)
-    for j, h, rows, keys, head in units:
+    def weigh_back(unit):
+        j, h, rows, keys, head = unit
+        return nt_dot(grad_attended_ref[rows, head], values_ref[keys, head])
+
+    ahead = [weigh_back(units[u]) for u in range(DEPTH)]
+    for u, (j, h, rows, keys, head) in enumerate(units):
         length = rows.stop - rows.start
-        grad_weights = nt_dot(grad_attended_ref[rows, head], values_ref[keys, head])
+        grad_weights = ahead.pop(0)
+        if u + DEPTH < len(units):
+            ahead.append(weigh_back(units[u + DEPTH]))
         grad_scores = (grad_weights * score_slope_ref[HEADS * j + h, :length, :]).astype(BF16)
         grad_queries_ref[rows, head] += jnp.dot(grad_scores, keys_ref[keys, head], preferred_element_type=F32)
         grad_values = jnp.dot(
@@ -405,6 +440,10 @@
     return blocks.reshape(TABLES, COLS * HALF, 128)
 
 
+def swap_cols(values, mask):
+    return lax.ppermute(values, "col", [(c, c ^ mask) for c in range(COLS)])
+
+
 def shards(table_rows, ada_state, w_uvqk, w_out, tok_owner, tok_slot, seg_ids, cotangent):
     def member():
         return lax.axis_index("col")
@@ -419,7 +458,8 @@
     layer_out, pieces = layer(received, place, member, seg_ids, w_uvqk, w_out, cotangent)
     arrived = exchange(pieces)
     grad_t, squares = add_rows(asked, arrived, parity)
-    squares = lax.all_to_all(squares, "col", split_axis=0, concat_axis=0, tiled=True)
+    squares = squares + swap_cols(squares, 1)
+    squares = [squares] + [swap_cols(squares, 2 * k) for k in range(1, COLS // 2)]
     new_table_t, new_state = update(
         squares, ada_state.reshape(TOUCH // 128, 128), table_t, grad_t
     )

time: 106 us -> 99.4 us (0.938)
  blocking collectives: 64.6 us -> 56.2 us
  Pallas kernels: 24.3 us -> 19.6 us
  starting transfers between devices: 7.58 us -> 12.1 us
  waiting for transfers between devices: 5.41 us -> 7.65 us
    all_to_all x1 -> x0, blocking collectives: 8.45 us -> none  [shards(): lax.all_to_all(squares, 'col', split_axis=0, concat_axis=0, tiled=True)]
    ppermute x0 -> x4, starting transfers between devices: none -> 4.56 us  [swap_cols(): return lax.ppermute(values, 'col', [(c, c ^ mask) for c in range(COLS)])]
    pallas_call x1, Pallas kernels: 14.3 us -> 10.9 us  [layer(): pl.pallas_call(functools.partial(layer_kernel, member), out_shape=(jax.Sh...]
    ppermute x0 -> x4, waiting for transfers between devices: none -> 2.24 us  [swap_cols(): return lax.ppermute(values, 'col', [(c, c ^ mask) for c in range(COLS)])]
  transfers between devices with their start and end apart: 1 -> 5, of which waited for: 1 -> 5; matrix products, arithmetic and copies ran while one was open for 0% -> 0% of each run, Pallas kernels for 0% -> 0%
where the time goes in v3:
time: 99.4 us; the launch traced here: 98.8 us
  blocking collectives  56.2 us (57%)
  Pallas kernels  19.6 us (20%)
  starting transfers between devices  12.1 us (12%)
  waiting for transfers between devices  7.65 us (8%)
  local copies, waits for them, and re-layouts  2.51 us (3%)
    all_to_all x2, blocking collectives, exchange(): lax.all_to_all(blocks, ('table', 'col'), split_axis=0, concat_axis=0, til...  56.2 us
    pallas_call x1, Pallas kernels, layer(): pl.pallas_call(functools.partial(layer_kernel, member), out_shape=(jax.Sh...  10.9 us
    all_to_all x1, starting transfers between devices, shards(): lax.all_to_all(asks, 'table', split_axis=0, concat_axis=0, tiled=True)  7.58 us
    all_to_all x1, waiting for transfers between devices, shards(): lax.all_to_all(asks, 'table', split_axis=0, concat_axis=0, tiled=True)  5.41 us
    ppermute x4, starting transfers between devices, swap_cols(): return lax.ppermute(values, 'col', [(c, c ^ mask) for c in range(COLS)])  4.56 us
    pallas_call x1, Pallas kernels, pick_rows(): pl.pallas_call(functools.partial(pick_kernel, parity), out_shape=jax.Shap...  3.24 us
    pallas_call x1, Pallas kernels, add_rows(): pl.pallas_call(functools.partial(add_kernel, parity), out_shape=(jax.Shap...  2.96 us
    unnamed x18, local copies, waits for them, and re-layouts  2.51 us
  transfers between devices with their start and end apart: 5, of which 5 were waited for; matrix products, arithmetic and copies ran while one was open for 0% of the time, Pallas kernels for 0%

profile of v3, /device:TPU:1, one launch (start us, length us, event | category | flops | bytes accessed | tf_op | source)
XLA Modules:
  0.0 98.8 jit_solution(17912160521810434386)
XLA Ops:
  0.6 0.0 copy-start.5
  0.6 0.7 copy-done.5
  1.4 0.0 copy-start.6
  1.4 0.7 copy-done.6
  2.1 1.6 %ask.1 = (s32[16,1,640]{2,1,0:T(1,128)}, s32[8,640]{1,0:T(8,128)S(1)}) custom-call(s32[1,5120]{1,0:T(1,128)S(1)} %bitcast.15, s32[1,5120]{1,0:T(1,128)S(1)} %copy-done.6), custom_call_target="tpu_custom_call" | custom-call | tf_op jit(solution)/shard_map/ask/pallas_call | solution.py:97
  3.7 7.6 %all-to-all-start = ((s32[16,1,640]{2,1,0:T(1,128)}), s32[16,1,640]{2,1,0:T(1,128)S(1)}, u32[]{:S(2)}, u32[]{:S(2)}) async-start(s32[16,1,640]{2,1,0:T(1,128)} %get-tuple-element.11), calls=%async_computation | async-start | bytes 81920 | tf_op jit(solution)/shard_map/all_to_all | solution.py:456
  11.2 0.0 copy-start.1
  11.3 1.0 %copy-done.1 = f32[2048,64]{0,1:T(8,128)S(1)} copy-done((f32[2048,64]{0,1:T(8,128)S(1)}, f32[2048,64]{0,1:T(8,128)}, u32[]{:S(2)}) %copy-start.1) | copy-done | bytes 524312
  12.3 5.4 %all-to-all-done.asks_ref = s32[16,1,640]{2,1,0:T(1,128)S(1)} async-done(((s32[16,1,640]{2,1,0:T(1,128)}), s32[16,1,640]{2,1,0:T(1,128)S(1)}, u32[]{:S(2)}, u32[]{:S(2)}) %all-to-all-start) | async-done | bytes 40992 | tf_op jit(solution)/shard_map/all_to_all | solution.py:456
  17.7 3.2 %pick.1 = bf16[16,320,128]{2,1,0:T(8,128)(2,1)S(1)} custom-call(s32[16,1,640]{2,1,0:T(1,128)S(1)} %all-to-all-done.asks_ref, bf16[512,256]{1,0:T(8,128)(2,1)S(1)} %rows.1.rows_ref), custom_call_target="tpu_custom_call" | custom-call | tf_op jit(solution)/shard_map/pick/pallas_call | solution.py:161
  21.0 0.0 copy-start
  21.0 0.0 copy-start.4
  21.0 0.0 copy-start.8
  21.0 30.0 %all_to_all.15 = bf16[128,40,128]{2,1,0:T(8,128)(2,1)S(1)} all-to-all(bf16[128,40,128]{2,1,0:T(8,128)(2,1)S(1)} %bitcast.11), channel_id=1, replica_groups=mesh['table'=16,'col'=8] {'table','col'}, dimensions={0} | all-to-all | bytes 2621440 | tf_op jit(solution)/shard_map/all_to_all | solution.py:439
  51.1 0.0 copy-done.3
  51.1 0.0 copy-done
  51.1 0.0 copy-done.4
  51.1 0.0 copy-done.8
  51.1 10.9 %layer.1 = (bf16[640,512]{1,0:T(8,128)(2,1)}, bf16[16,320,128]{2,1,0:T(8,128)(2,1)S(1)}) custom-call(bf16[16,320,128]{2,1,0:T(8,128)(2,1)S(1)} %bitcast.9, s32[8,640]{1,0:T(8,128)S(1)} %get-tuple-element.12.place_ref, s32[1,640]{1,0:T(1,128)S(1)} %copy-done.8, bf16[512,2048]{1,0:T(8,128)(2,1)S(1)} %copy-done, bf16[512,512]{1,0:T(8,128)(2,1)S(1)} %copy-done.4, ...), custom_call_target="tpu_custom_call" | custom-call | tf_op jit(solution)/shard_map/layer/pallas_call | solution.py:408
  62.0 26.1 %all_to_all.16 = bf16[128,40,128]{2,1,0:T(8,128)(2,1)S(1)} all-to-all(bf16[128,40,128]{2,1,0:T(8,128)(2,1)S(1)} %bitcast.14), channel_id=1, replica_groups=mesh['table'=16,'col'=8] {'table','col'}, dimensions={0} | all-to-all | bytes 2621440 | tf_op jit(solution)/shard_map/all_to_all | solution.py:439
  88.1 3.0 %add.5 = (f32[64,2048]{1,0:T(8,128)S(1)}, f32[16,128]{1,0:T(8,128)S(1)}) custom-call(s32[16,1,640]{2,1,0:T(1,128)S(1)} %all-to-all-done.asks_ref, bf16[16,320,128]{2,1,0:T(8,128)(2,1)S(1)} %bitcast.10), custom_call_target="tpu_custom_call" | custom-call | tf_op jit(solution)/shard_map/add/pallas_call | solution.py:198
  91.1 1.3 %collective-permute-start = (f32[16,128]{1,0:T(8,128)S(1)}, f32[16,128]{1,0:T(8,128)S(1)}, u32[]{:S(2)}, u32[]{:S(2)}) collective-permute-start(f32[16,128]{1,0:T(8,128)S(1)} %get-tuple-element.15), channel_id=1, source_target_pairs={{0,1},{1,0},{2,3},{3,2},{4,5},{5,4},{6,7},{7,6},{8,9},{9,8},{10,11... | collective-permute-start | bytes 24584 | tf_op jit(solution)/shard_map/ppermute | solution.py:444
  92.4 0.8 collective-permute-done
  93.2 0.0 collective-permute-start.3
  93.2 1.8 %collective-permute-start.2 = (f32[16,128]{1,0:T(8,128)S(1)}, f32[16,128]{1,0:T(8,128)S(1)}, u32[]{:S(2)}, u32[]{:S(2)}) collective-permute-start(f32[16,128]{1,0:T(8,128)S(1)} %add.4.own_ref), channel_id=1, source_target_pairs={{0,4},{1,5},{2,6},{3,7},{4,0},{5,1},{6,2},{7,3},{8,12},{9,13},{10,... | collective-permute-start | bytes 24584 | tf_op jit(solution)/shard_map/ppermute | solution.py:444
  95.0 1.4 %collective-permute-start.1 = (f32[16,128]{1,0:T(8,128)S(1)}, f32[16,128]{1,0:T(8,128)S(1)}, u32[]{:S(2)}, u32[]{:S(2)}) collective-permute-start(f32[16,128]{1,0:T(8,128)S(1)} %add.4.own_ref), channel_id=1, source_target_pairs={{0,2},{1,3},{2,0},{3,1},{4,6},{5,7},{6,4},{7,5},{8,10},{9,11},{10,... | collective-permute-start | bytes 24584 | tf_op jit(solution)/shard_map/ppermute | solution.py:444
  96.5 0.5 collective-permute-done.3.last_ref
  96.9 0.3 collective-permute-done.2.far_ref
  97.2 0.7 collective-permute-done.1.near_ref
  97.9 0.0 copy-done.2
  97.9 0.0 copy-done.7
  97.9 0.9 update.1
  (5 shorter events, 0.0 us)
Async XLA Ops:
  0.6 0.7 copy-start.5
  1.4 0.7 copy-start.6
  3.7 14.1 %all-to-all-start = ((s32[16,1,640]{2,1,0:T(1,128)}), s32[16,1,640]{2,1,0:T(1,128)S(1)}, u32[]{:S(2)}, u32[]{:S(2)}) async-start(s32[16,1,640]{2,1,0:T(1,128)} %get-tuple-element.11), calls=%async_computation | async-start | bytes 81920 | tf_op jit(solution)/shard_map/all_to_all | solution.py:456
  11.2 1.0 %copy-start.1 = (f32[2048,64]{0,1:T(8,128)S(1)}, f32[2048,64]{0,1:T(8,128)}, u32[]{:S(2)}) copy-start(f32[2048,64]{0,1:T(8,128)} %param.8) | copy-start | bytes 1572868
  17.7 33.3 %copy-start.3 = (bf16[640,512]{1,0:T(8,128)(2,1)S(1)}, bf16[640,512]{1,0:T(8,128)(2,1)}, u32[]{:S(2)}) copy-start(bf16[640,512]{1,0:T(8,128)(2,1)} %cotangent_ref.1) | copy-start | bytes 1966084
  21.0 30.1 %copy-start = (bf16[512,2048]{1,0:T(8,128)(2,1)S(1)}, bf16[512,2048]{1,0:T(8,128)(2,1)}, u32[]{:S(2)}) copy-start(bf16[512,2048]{1,0:T(8,128)(2,1)} %w_ref.1) | copy-start | bytes 6291460
  21.0 30.1 %copy-start.4 = (bf16[512,512]{1,0:T(8,128)(2,1)S(1)}, bf16[512,512]{1,0:T(8,128)(2,1)}, u32[]{:S(2)}) copy-start(bf16[512,512]{1,0:T(8,128)(2,1)} %w_out_ref.1) | copy-start | bytes 1572868
  21.0 30.1 %copy-start.8 = (s32[1,640]{1,0:T(1,128)S(1)}, s32[1,640]{1,0:T(1,128)}, u32[]{:S(2)}) copy-start(s32[1,640]{1,0:T(1,128)} %segment_ref.1) | copy-start | bytes 7684
  88.1 9.8 %copy-start.2 = (f32[2048,64]{0,1:T(8,128)S(1)}, f32[2048,64]{0,1:T(8,128)}, u32[]{:S(2)}) copy-start(f32[2048,64]{0,1:T(8,128)} %param.8) | copy-start | bytes 1572868
  88.1 9.8 %copy-start.7 = (f32[2048]{0:T(1024)S(1)}, f32[2048]{0:T(1024)}, u32[]{:S(2)}) copy-start(f32[2048]{0:T(1024)} %param.9) | copy-start | bytes 24580
  91.1 2.1 %collective-permute-start = (f32[16,128]{1,0:T(8,128)S(1)}, f32[16,128]{1,0:T(8,128)S(1)}, u32[]{:S(2)}, u32[]{:S(2)}) collective-permute-start(f32[16,128]{1,0:T(8,128)S(1)} %get-tuple-element.15), channel_id=1, source_target_pairs={{0,1},{1,0},{2,3},{3,2},{4,5},{5,4},{6,7},{7,6},{8,9},{9,8},{10,11... | collective-permute-start | bytes 24584 | tf_op jit(solution)/shard_map/ppermute | solution.py:444
  93.2 3.7 %collective-permute-start.3 = (f32[16,128]{1,0:T(8,128)S(1)}, f32[16,128]{1,0:T(8,128)S(1)}, u32[]{:S(2)}, u32[]{:S(2)}) collective-permute-start(f32[16,128]{1,0:T(8,128)S(1)} %add.4.own_ref), channel_id=1, source_target_pairs={{0,6},{1,7},{2,4},{3,5},{4,2},{5,3},{6,0},{7,1},{8,14},{9,15},{10,... | collective-permute-start | bytes 24584 | tf_op jit(solution)/shard_map/ppermute | solution.py:444
  93.2 4.0 %collective-permute-start.2 = (f32[16,128]{1,0:T(8,128)S(1)}, f32[16,128]{1,0:T(8,128)S(1)}, u32[]{:S(2)}, u32[]{:S(2)}) collective-permute-start(f32[16,128]{1,0:T(8,128)S(1)} %add.4.own_ref), channel_id=1, source_target_pairs={{0,4},{1,5},{2,6},{3,7},{4,0},{5,1},{6,2},{7,3},{8,12},{9,13},{10,... | collective-permute-start | bytes 24584 | tf_op jit(solution)/shard_map/ppermute | solution.py:444
  95.0 2.9 %collective-permute-start.1 = (f32[16,128]{1,0:T(8,128)S(1)}, f32[16,128]{1,0:T(8,128)S(1)}, u32[]{:S(2)}, u32[]{:S(2)}) collective-permute-start(f32[16,128]{1,0:T(8,128)S(1)} %add.4.own_ref), channel_id=1, source_target_pairs={{0,2},{1,3},{2,0},{3,1},{4,6},{5,7},{6,4},{7,5},{8,10},{9,11},{10,... | collective-permute-start | bytes 24584 | tf_op jit(solution)/shard_map/ppermute | solution.py:444

commit v4 on v3

--- a/solution.py
+++ b/solution.py
@@ -26,7 +26,7 @@
 DEPTH = 2
 PAIR = 2 * ASKS
 REACH_TILES = 384
-FAR = -1.0e4
+FAR = -64.0
 
 NORM_EPS = 1e-05
 ROOT_EPS = 1e-08
@@ -100,7 +100,6 @@
             jax.ShapeDtypeStruct((TABLES, 1, ASKS), I32),
             jax.ShapeDtypeStruct((COLS, TOK_DEV), I32),
         ),
-        compiler_params=params(16),
         name="ask",
     )(owner, slot)
 

time: 99.4 us -> 99 us (level)
  local copies, waits for them, and re-layouts: 2.51 us -> 1.07 us
  Pallas kernels: 19.6 us -> 20.6 us
    unnamed x18 -> x16, local copies, waits for them, and re-layouts: 2.51 us -> 1.07 us
where the time goes in v4:
time: 99 us; the launch traced here: 98.4 us
  blocking collectives  56.2 us (57%)
  Pallas kernels  20.6 us (21%)
  starting transfers between devices  12.1 us (12%)
  waiting for transfers between devices  7.65 us (8%)
  local copies, waits for them, and re-layouts  1.07 us (1%)
    all_to_all x2, blocking collectives, exchange(): lax.all_to_all(blocks, ('table', 'col'), split_axis=0, concat_axis=0, til...  56.2 us
    pallas_call x1, Pallas kernels, layer(): pl.pallas_call(functools.partial(layer_kernel, member), out_shape=(jax.Sh...  10.9 us
    all_to_all x1, starting transfers between devices, shards(): lax.all_to_all(asks, 'table', split_axis=0, concat_axis=0, tiled=True)  7.58 us
    all_to_all x1, waiting for transfers between devices, shards(): lax.all_to_all(asks, 'table', split_axis=0, concat_axis=0, tiled=True)  5.41 us
    ppermute x4, starting transfers between devices, swap_cols(): return lax.ppermute(values, 'col', [(c, c ^ mask) for c in range(COLS)])  4.56 us
    pallas_call x1, Pallas kernels, pick_rows(): pl.pallas_call(functools.partial(pick_kernel, parity), out_shape=jax.Shap...  3.52 us
    pallas_call x1, Pallas kernels, add_rows(): pl.pallas_call(functools.partial(add_kernel, parity), out_shape=(jax.Shap...  2.95 us
    pallas_call x1, Pallas kernels, make_asks(): pl.pallas_call(ask_kernel, out_shape=(jax.ShapeDtypeStruct((TABLES, 1, AS...  2.32 us
  transfers between devices with their start and end apart: 5, of which 5 were waited for; matrix products, arithmetic and copies ran while one was open for 0% of the time, Pallas kernels for 0%

profile of v4, /device:TPU:1, one launch (start us, length us, event | category | flops | bytes accessed | tf_op | source)
XLA Modules:
  0.0 98.4 jit_solution(4573247932889232480)
XLA Ops:
  0.6 2.3 %ask.1 = (s32[16,1,640]{2,1,0:T(1,128)}, s32[8,640]{1,0:T(8,128)}) custom-call(s32[1,5120]{1,0:T(1,128)} %bitcast.16, s32[1,5120]{1,0:T(1,128)} %slot_ref.1), custom_call_target="tpu_custom_call" | custom-call | tf_op jit(solution)/shard_map/ask/pallas_call | solution.py:97
  2.9 7.6 %all-to-all-start = ((s32[16,1,640]{2,1,0:T(1,128)}), s32[16,1,640]{2,1,0:T(1,128)S(1)}, u32[]{:S(2)}, u32[]{:S(2)}) async-start(s32[16,1,640]{2,1,0:T(1,128)} %get-tuple-element.11), calls=%async_computation | async-start | bytes 81920 | tf_op jit(solution)/shard_map/all_to_all | solution.py:455
  10.5 0.0 copy-start.1
  10.5 1.0 %copy-done.1 = f32[2048,64]{0,1:T(8,128)S(1)} copy-done((f32[2048,64]{0,1:T(8,128)S(1)}, f32[2048,64]{0,1:T(8,128)}, u32[]{:S(2)}) %copy-start.1) | copy-done | bytes 524312
  11.6 5.4 %all-to-all-done.asks_ref = s32[16,1,640]{2,1,0:T(1,128)S(1)} async-done(((s32[16,1,640]{2,1,0:T(1,128)}), s32[16,1,640]{2,1,0:T(1,128)S(1)}, u32[]{:S(2)}, u32[]{:S(2)}) %all-to-all-start) | async-done | bytes 40992 | tf_op jit(solution)/shard_map/all_to_all | solution.py:455
  17.0 0.0 copy-start.3
  17.0 0.0 copy-start.5
  17.0 3.5 %pick.1 = bf16[16,320,128]{2,1,0:T(8,128)(2,1)S(1)} custom-call(s32[16,1,640]{2,1,0:T(1,128)S(1)} %all-to-all-done.asks_ref, bf16[512,256]{1,0:T(8,128)(2,1)S(1)} %rows.1.rows_ref), custom_call_target="tpu_custom_call" | custom-call | tf_op jit(solution)/shard_map/pick/pallas_call | solution.py:160
  20.5 0.0 copy-start
  20.6 0.0 copy-start.4
  20.6 0.0 copy-start.7
  20.6 30.1 %all_to_all.15 = bf16[128,40,128]{2,1,0:T(8,128)(2,1)S(1)} all-to-all(bf16[128,40,128]{2,1,0:T(8,128)(2,1)S(1)} %bitcast.11), channel_id=1, replica_groups=mesh['table'=16,'col'=8] {'table','col'}, dimensions={0} | all-to-all | bytes 2621440 | tf_op jit(solution)/shard_map/all_to_all | solution.py:438
  50.6 0.0 copy-done.3
  50.6 0.0 copy-done.5
  50.6 0.0 copy-done
  50.6 0.0 copy-done.4
  50.7 0.0 copy-done.7
  50.7 10.9 %layer.1 = (bf16[640,512]{1,0:T(8,128)(2,1)}, bf16[16,320,128]{2,1,0:T(8,128)(2,1)S(1)}) custom-call(bf16[16,320,128]{2,1,0:T(8,128)(2,1)S(1)} %bitcast.9, s32[8,640]{1,0:T(8,128)S(1)} %copy-done.5, s32[1,640]{1,0:T(1,128)S(1)} %copy-done.7, bf16[512,2048]{1,0:T(8,128)(2,1)S(1)} %copy-done, bf16[512,512]{1,0:T(8,128)(2,1)S(1)} %copy-done.4, ...), custom_call_target="tpu_custom_call" | custom-call | tf_op jit(solution)/shard_map/layer/pallas_call | solution.py:407
  61.6 26.1 %all_to_all.16 = bf16[128,40,128]{2,1,0:T(8,128)(2,1)S(1)} all-to-all(bf16[128,40,128]{2,1,0:T(8,128)(2,1)S(1)} %bitcast.14), channel_id=1, replica_groups=mesh['table'=16,'col'=8] {'table','col'}, dimensions={0} | all-to-all | bytes 2621440 | tf_op jit(solution)/shard_map/all_to_all | solution.py:438
  87.7 0.0 copy-start.2
  87.7 3.0 %add.5 = (f32[64,2048]{1,0:T(8,128)S(1)}, f32[16,128]{1,0:T(8,128)S(1)}) custom-call(s32[16,1,640]{2,1,0:T(1,128)S(1)} %all-to-all-done.asks_ref, bf16[16,320,128]{2,1,0:T(8,128)(2,1)S(1)} %bitcast.10), custom_call_target="tpu_custom_call" | custom-call | tf_op jit(solution)/shard_map/add/pallas_call | solution.py:197
  90.7 1.3 %collective-permute-start = (f32[16,128]{1,0:T(8,128)S(1)}, f32[16,128]{1,0:T(8,128)S(1)}, u32[]{:S(2)}, u32[]{:S(2)}) collective-permute-start(f32[16,128]{1,0:T(8,128)S(1)} %get-tuple-element.15), channel_id=1, source_target_pairs={{0,1},{1,0},{2,3},{3,2},{4,5},{5,4},{6,7},{7,6},{8,9},{9,8},{10,11... | collective-permute-start | bytes 24584 | tf_op jit(solution)/shard_map/ppermute | solution.py:443
  92.0 0.8 collective-permute-done
  92.8 0.0 collective-permute-start.3
  92.8 1.8 %collective-permute-start.2 = (f32[16,128]{1,0:T(8,128)S(1)}, f32[16,128]{1,0:T(8,128)S(1)}, u32[]{:S(2)}, u32[]{:S(2)}) collective-permute-start(f32[16,128]{1,0:T(8,128)S(1)} %add.4.own_ref), channel_id=1, source_target_pairs={{0,4},{1,5},{2,6},{3,7},{4,0},{5,1},{6,2},{7,3},{8,12},{9,13},{10,... | collective-permute-start | bytes 24584 | tf_op jit(solution)/shard_map/ppermute | solution.py:443
  94.6 1.4 %collective-permute-start.1 = (f32[16,128]{1,0:T(8,128)S(1)}, f32[16,128]{1,0:T(8,128)S(1)}, u32[]{:S(2)}, u32[]{:S(2)}) collective-permute-start(f32[16,128]{1,0:T(8,128)S(1)} %add.4.own_ref), channel_id=1, source_target_pairs={{0,2},{1,3},{2,0},{3,1},{4,6},{5,7},{6,4},{7,5},{8,10},{9,11},{10,... | collective-permute-start | bytes 24584 | tf_op jit(solution)/shard_map/ppermute | solution.py:443
  96.1 0.5 collective-permute-done.3.last_ref
  96.5 0.3 collective-permute-done.2.far_ref
  96.8 0.7 collective-permute-done.1.near_ref
  97.5 0.0 copy-done.2
  97.5 0.0 copy-done.6
  97.5 0.9 update.1
  (3 shorter events, 0.0 us)
Async XLA Ops:
  2.9 14.1 %all-to-all-start = ((s32[16,1,640]{2,1,0:T(1,128)}), s32[16,1,640]{2,1,0:T(1,128)S(1)}, u32[]{:S(2)}, u32[]{:S(2)}) async-start(s32[16,1,640]{2,1,0:T(1,128)} %get-tuple-element.11), calls=%async_computation | async-start | bytes 81920 | tf_op jit(solution)/shard_map/all_to_all | solution.py:455
  10.5 1.0 %copy-start.1 = (f32[2048,64]{0,1:T(8,128)S(1)}, f32[2048,64]{0,1:T(8,128)}, u32[]{:S(2)}) copy-start(f32[2048,64]{0,1:T(8,128)} %param.8) | copy-start | bytes 1572868
  17.0 33.6 %copy-start.3 = (bf16[640,512]{1,0:T(8,128)(2,1)S(1)}, bf16[640,512]{1,0:T(8,128)(2,1)}, u32[]{:S(2)}) copy-start(bf16[640,512]{1,0:T(8,128)(2,1)} %cotangent_ref.1) | copy-start | bytes 1966084
  17.0 33.6 %copy-start.5 = (s32[8,640]{1,0:T(8,128)S(1)}, s32[8,640]{1,0:T(8,128)}, u32[]{:S(2)}) copy-start(s32[8,640]{1,0:T(8,128)} %get-tuple-element.12.place_ref) | copy-start | bytes 61444
  20.5 30.1 %copy-start = (bf16[512,2048]{1,0:T(8,128)(2,1)S(1)}, bf16[512,2048]{1,0:T(8,128)(2,1)}, u32[]{:S(2)}) copy-start(bf16[512,2048]{1,0:T(8,128)(2,1)} %w_ref.1) | copy-start | bytes 6291460
  20.6 30.1 %copy-start.4 = (bf16[512,512]{1,0:T(8,128)(2,1)S(1)}, bf16[512,512]{1,0:T(8,128)(2,1)}, u32[]{:S(2)}) copy-start(bf16[512,512]{1,0:T(8,128)(2,1)} %w_out_ref.1) | copy-start | bytes 1572868
  20.6 30.1 %copy-start.7 = (s32[1,640]{1,0:T(1,128)S(1)}, s32[1,640]{1,0:T(1,128)}, u32[]{:S(2)}) copy-start(s32[1,640]{1,0:T(1,128)} %segment_ref.1) | copy-start | bytes 7684
  87.7 9.8 %copy-start.2 = (f32[2048,64]{0,1:T(8,128)S(1)}, f32[2048,64]{0,1:T(8,128)}, u32[]{:S(2)}) copy-start(f32[2048,64]{0,1:T(8,128)} %param.8) | copy-start | bytes 1572868
  87.7 9.8 %copy-start.6 = (f32[2048]{0:T(1024)S(1)}, f32[2048]{0:T(1024)}, u32[]{:S(2)}) copy-start(f32[2048]{0:T(1024)} %param.9) | copy-start | bytes 24580
  90.7 2.1 %collective-permute-start = (f32[16,128]{1,0:T(8,128)S(1)}, f32[16,128]{1,0:T(8,128)S(1)}, u32[]{:S(2)}, u32[]{:S(2)}) collective-permute-start(f32[16,128]{1,0:T(8,128)S(1)} %get-tuple-element.15), channel_id=1, source_target_pairs={{0,1},{1,0},{2,3},{3,2},{4,5},{5,4},{6,7},{7,6},{8,9},{9,8},{10,11... | collective-permute-start | bytes 24584 | tf_op jit(solution)/shard_map/ppermute | solution.py:443
  92.8 3.7 %collective-permute-start.3 = (f32[16,128]{1,0:T(8,128)S(1)}, f32[16,128]{1,0:T(8,128)S(1)}, u32[]{:S(2)}, u32[]{:S(2)}) collective-permute-start(f32[16,128]{1,0:T(8,128)S(1)} %add.4.own_ref), channel_id=1, source_target_pairs={{0,6},{1,7},{2,4},{3,5},{4,2},{5,3},{6,0},{7,1},{8,14},{9,15},{10,... | collective-permute-start | bytes 24584 | tf_op jit(solution)/shard_map/ppermute | solution.py:443
  92.8 4.0 %collective-permute-start.2 = (f32[16,128]{1,0:T(8,128)S(1)}, f32[16,128]{1,0:T(8,128)S(1)}, u32[]{:S(2)}, u32[]{:S(2)}) collective-permute-start(f32[16,128]{1,0:T(8,128)S(1)} %add.4.own_ref), channel_id=1, source_target_pairs={{0,4},{1,5},{2,6},{3,7},{4,0},{5,1},{6,2},{7,3},{8,12},{9,13},{10,... | collective-permute-start | bytes 24584 | tf_op jit(solution)/shard_map/ppermute | solution.py:443
  94.6 2.9 %collective-permute-start.1 = (f32[16,128]{1,0:T(8,128)S(1)}, f32[16,128]{1,0:T(8,128)S(1)}, u32[]{:S(2)}, u32[]{:S(2)}) collective-permute-start(f32[16,128]{1,0:T(8,128)S(1)} %add.4.own_ref), channel_id=1, source_target_pairs={{0,2},{1,3},{2,0},{3,1},{4,6},{5,7},{6,4},{7,5},{8,10},{9,11},{10,... | collective-permute-start | bytes 24584 | tf_op jit(solution)/shard_map/ppermute | solution.py:443

commit v5 on v4

--- a/solution.py
+++ b/solution.py
@@ -63,11 +63,18 @@
 
 
 def ask_kernel(owner_ref, slot_ref, asks_ref, place_ref):
-    lower = jnp.where(iota((TOK_DEV, TOK_DEV), 0) <= iota((TOK_DEV, TOK_DEV), 1), 1.0, 0.0).astype(BF16)
+    lower = jnp.where(iota((128, 128), 0) <= iota((128, 128), 1), 1.0, 0.0).astype(BF16)
     hits = hits_of(owner_ref)
-    running = jnp.dot(
-        jnp.concatenate(hits, axis=0).astype(BF16), lower, preferred_element_type=F32
-    )
+    chunks = [slice(128 * j, 128 * (j + 1)) for j in range(TOK_DEV // 128)]
+    stacked = jnp.concatenate([hit[:, chunk] for chunk in chunks for hit in hits], axis=0)
+    within = jnp.dot(stacked.astype(BF16), lower, preferred_element_type=F32)
+    before = jnp.zeros((COLS * TABLES, 1), F32)
+    running = []
+    for j in range(len(chunks)):
+        part = within[COLS * TABLES * j : COLS * TABLES * (j + 1)]
+        running.append(part + before)
+        before = before + part[:, 127:]
+    running = jnp.concatenate(running, axis=1)
     lane = iota((TABLES, 128), 1)
     slot_at = iota((128, TOK_DEV), 0)
     tiles = [jnp.zeros((TABLES, 128), F32) for _ in range(ASKS // 128)]
@@ -251,8 +258,10 @@
     w_ref,
     w_out_ref,
     cotangent_ref,
+    out_hbm,
+    pieces_ref,
     out_ref,
-    pieces_ref,
+    left_sem,
     slots_ref,
     segment_col,
     embedded_ref,
@@ -355,6 +364,8 @@
     gated = (again * gates_ref[...]).astype(BF16)
     out = jnp.dot(gated, w_out_ref[...], preferred_element_type=F32)
     out_ref[...] = (out + embedded_ref[...].astype(F32)).astype(BF16)
+    leaving = pltpu.make_async_copy(out_ref, out_hbm, left_sem)
+    leaving.start()
     grad_gated = nt_dot(cotangent_ref[...], w_out_ref[...]).astype(BF16).astype(F32)
     grad_u_ref[:, :D] = (grad_gated * again * slope_ref[:, :D]).astype(BF16)
     grad_attended_ref[...] = normalise_back(grad_gated * gates_ref[...], again, root_again).astype(BF16)
@@ -400,6 +411,7 @@
             pieces_ref[t, 2 * HALF * j : 2 * HALF * (j + 1), :] = jnp.concatenate(
                 [even[rows], odd[rows]], axis=0
             ).astype(BF16)
+    leaving.wait()
 
 
 def layer(received, place, member, segment, w_uvqk, w_out, cotangent):
@@ -410,7 +422,10 @@
             jax.ShapeDtypeStruct((TOK_DEV, D), BF16),
             jax.ShapeDtypeStruct((TABLES, COLS * HALF, 128), BF16),
         ),
+        out_specs=(pl.BlockSpec(memory_space=pl.ANY), pl.BlockSpec(memory_space=pltpu.VMEM)),
         scratch_shapes=[
+            pltpu.VMEM((TOK_DEV, D), BF16),
+            pltpu.SemaphoreType.DMA,
             pltpu.VMEM((TABLES * CAP, D), BF16),
             pltpu.VMEM((TOK_DEV, 128), F32),
             pltpu.VMEM((TOK_DEV, D), BF16),

time: 99 us -> 98.9 us (level)
  no operation moved by 1% of the time
where the time goes in v5:
time: 98.9 us; the launch traced here: 98.3 us
  blocking collectives  56.2 us (57%)
  Pallas kernels  20.6 us (21%)
  starting transfers between devices  12.1 us (12%)
  waiting for transfers between devices  7.65 us (8%)
  local copies, waits for them, and re-layouts  1.07 us (1%)
    all_to_all x2, blocking collectives, exchange(): lax.all_to_all(blocks, ('table', 'col'), split_axis=0, concat_axis=0, til...  56.2 us
    pallas_call x1, Pallas kernels, layer(): pl.pallas_call(functools.partial(layer_kernel, member), out_shape=(jax.Sh...  10.9 us
    all_to_all x1, starting transfers between devices, shards(): lax.all_to_all(asks, 'table', split_axis=0, concat_axis=0, tiled=True)  7.58 us
    all_to_all x1, waiting for transfers between devices, shards(): lax.all_to_all(asks, 'table', split_axis=0, concat_axis=0, tiled=True)  5.4 us
    ppermute x4, starting transfers between devices, swap_cols(): return lax.ppermute(values, 'col', [(c, c ^ mask) for c in range(COLS)])  4.56 us
    pallas_call x1, Pallas kernels, pick_rows(): pl.pallas_call(functools.partial(pick_kernel, parity), out_shape=jax.Shap...  3.52 us
    pallas_call x1, Pallas kernels, add_rows(): pl.pallas_call(functools.partial(add_kernel, parity), out_shape=(jax.Shap...  2.95 us
    pallas_call x1, Pallas kernels, make_asks(): pl.pallas_call(ask_kernel, out_shape=(jax.ShapeDtypeStruct((TABLES, 1, AS...  2.26 us
  transfers between devices with their start and end apart: 5, of which 5 were waited for; matrix products, arithmetic and copies ran while one was open for 0% of the time, Pallas kernels for 0%

profile of v5, /device:TPU:1, one launch (start us, length us, event | category | flops | bytes accessed | tf_op | source)
XLA Modules:
  0.0 98.3 jit_solution(147393373877414687)
XLA Ops:
  0.6 2.3 %ask.1 = (s32[16,1,640]{2,1,0:T(1,128)}, s32[8,640]{1,0:T(8,128)}) custom-call(s32[1,5120]{1,0:T(1,128)} %bitcast.16, s32[1,5120]{1,0:T(1,128)} %slot_ref.1), custom_call_target="tpu_custom_call" | custom-call | tf_op jit(solution)/shard_map/ask/pallas_call | solution.py:104
  2.9 7.6 %all-to-all-start = ((s32[16,1,640]{2,1,0:T(1,128)}), s32[16,1,640]{2,1,0:T(1,128)S(1)}, u32[]{:S(2)}, u32[]{:S(2)}) async-start(s32[16,1,640]{2,1,0:T(1,128)} %get-tuple-element.11), calls=%async_computation | async-start | bytes 81920 | tf_op jit(solution)/shard_map/all_to_all | solution.py:470
  10.5 0.0 copy-start.1
  10.5 1.0 %copy-done.1 = f32[2048,64]{0,1:T(8,128)S(1)} copy-done((f32[2048,64]{0,1:T(8,128)S(1)}, f32[2048,64]{0,1:T(8,128)}, u32[]{:S(2)}) %copy-start.1) | copy-done | bytes 524312
  11.6 5.4 %all-to-all-done.asks_ref = s32[16,1,640]{2,1,0:T(1,128)S(1)} async-done(((s32[16,1,640]{2,1,0:T(1,128)}), s32[16,1,640]{2,1,0:T(1,128)S(1)}, u32[]{:S(2)}, u32[]{:S(2)}) %all-to-all-start) | async-done | bytes 40992 | tf_op jit(solution)/shard_map/all_to_all | solution.py:470
  17.0 0.0 copy-start.3
  17.0 0.0 copy-start.5
  17.0 3.5 %pick.1 = bf16[16,320,128]{2,1,0:T(8,128)(2,1)S(1)} custom-call(s32[16,1,640]{2,1,0:T(1,128)S(1)} %all-to-all-done.asks_ref, bf16[512,256]{1,0:T(8,128)(2,1)S(1)} %rows.1.rows_ref), custom_call_target="tpu_custom_call" | custom-call | tf_op jit(solution)/shard_map/pick/pallas_call | solution.py:167
  20.5 0.0 copy-start
  20.5 0.0 copy-start.4
  20.5 0.0 copy-start.7
  20.5 30.1 %all_to_all.15 = bf16[128,40,128]{2,1,0:T(8,128)(2,1)S(1)} all-to-all(bf16[128,40,128]{2,1,0:T(8,128)(2,1)S(1)} %bitcast.11), channel_id=1, replica_groups=mesh['table'=16,'col'=8] {'table','col'}, dimensions={0} | all-to-all | bytes 2621440 | tf_op jit(solution)/shard_map/all_to_all | solution.py:453
  50.6 0.0 copy-done.3
  50.6 0.0 copy-done.5
  50.6 0.0 copy-done
  50.6 0.0 copy-done.4
  50.6 0.0 copy-done.7
  50.6 10.9 %layer.1 = (bf16[640,512]{1,0:T(8,128)(2,1)}, bf16[16,320,128]{2,1,0:T(8,128)(2,1)S(1)}) custom-call(bf16[16,320,128]{2,1,0:T(8,128)(2,1)S(1)} %bitcast.9, s32[8,640]{1,0:T(8,128)S(1)} %copy-done.5, s32[1,640]{1,0:T(1,128)S(1)} %copy-done.7, bf16[512,2048]{1,0:T(8,128)(2,1)S(1)} %copy-done, bf16[512,512]{1,0:T(8,128)(2,1)S(1)} %copy-done.4, ...), custom_call_target="tpu_custom_call" | custom-call | tf_op jit(solution)/shard_map/layer/pallas_call | solution.py:419
  61.6 26.1 %all_to_all.16 = bf16[128,40,128]{2,1,0:T(8,128)(2,1)S(1)} all-to-all(bf16[128,40,128]{2,1,0:T(8,128)(2,1)S(1)} %bitcast.14), channel_id=1, replica_groups=mesh['table'=16,'col'=8] {'table','col'}, dimensions={0} | all-to-all | bytes 2621440 | tf_op jit(solution)/shard_map/all_to_all | solution.py:453
  87.7 0.0 copy-start.2
  87.7 3.0 %add.5 = (f32[64,2048]{1,0:T(8,128)S(1)}, f32[16,128]{1,0:T(8,128)S(1)}) custom-call(s32[16,1,640]{2,1,0:T(1,128)S(1)} %all-to-all-done.asks_ref, bf16[16,320,128]{2,1,0:T(8,128)(2,1)S(1)} %bitcast.10), custom_call_target="tpu_custom_call" | custom-call | tf_op jit(solution)/shard_map/add/pallas_call | solution.py:204
  90.6 1.3 %collective-permute-start = (f32[16,128]{1,0:T(8,128)S(1)}, f32[16,128]{1,0:T(8,128)S(1)}, u32[]{:S(2)}, u32[]{:S(2)}) collective-permute-start(f32[16,128]{1,0:T(8,128)S(1)} %get-tuple-element.15), channel_id=1, source_target_pairs={{0,1},{1,0},{2,3},{3,2},{4,5},{5,4},{6,7},{7,6},{8,9},{9,8},{10,11... | collective-permute-start | bytes 24584 | tf_op jit(solution)/shard_map/ppermute | solution.py:458
  91.9 0.8 collective-permute-done
  92.8 0.0 collective-permute-start.3
  92.8 1.8 %collective-permute-start.2 = (f32[16,128]{1,0:T(8,128)S(1)}, f32[16,128]{1,0:T(8,128)S(1)}, u32[]{:S(2)}, u32[]{:S(2)}) collective-permute-start(f32[16,128]{1,0:T(8,128)S(1)} %add.4.own_ref), channel_id=1, source_target_pairs={{0,4},{1,5},{2,6},{3,7},{4,0},{5,1},{6,2},{7,3},{8,12},{9,13},{10,... | collective-permute-start | bytes 24584 | tf_op jit(solution)/shard_map/ppermute | solution.py:458
  94.6 1.4 %collective-permute-start.1 = (f32[16,128]{1,0:T(8,128)S(1)}, f32[16,128]{1,0:T(8,128)S(1)}, u32[]{:S(2)}, u32[]{:S(2)}) collective-permute-start(f32[16,128]{1,0:T(8,128)S(1)} %add.4.own_ref), channel_id=1, source_target_pairs={{0,2},{1,3},{2,0},{3,1},{4,6},{5,7},{6,4},{7,5},{8,10},{9,11},{10,... | collective-permute-start | bytes 24584 | tf_op jit(solution)/shard_map/ppermute | solution.py:458
  96.0 0.5 collective-permute-done.3.last_ref
  96.5 0.3 collective-permute-done.2.far_ref
  96.8 0.7 collective-permute-done.1.near_ref
  97.4 0.0 copy-done.2
  97.4 0.0 copy-done.6
  97.4 0.9 update.1
  (3 shorter events, 0.0 us)
Async XLA Ops:
  2.9 14.1 %all-to-all-start = ((s32[16,1,640]{2,1,0:T(1,128)}), s32[16,1,640]{2,1,0:T(1,128)S(1)}, u32[]{:S(2)}, u32[]{:S(2)}) async-start(s32[16,1,640]{2,1,0:T(1,128)} %get-tuple-element.11), calls=%async_computation | async-start | bytes 81920 | tf_op jit(solution)/shard_map/all_to_all | solution.py:470
  10.5 1.0 %copy-start.1 = (f32[2048,64]{0,1:T(8,128)S(1)}, f32[2048,64]{0,1:T(8,128)}, u32[]{:S(2)}) copy-start(f32[2048,64]{0,1:T(8,128)} %param.8) | copy-start | bytes 1572868
  17.0 33.6 %copy-start.3 = (bf16[640,512]{1,0:T(8,128)(2,1)S(1)}, bf16[640,512]{1,0:T(8,128)(2,1)}, u32[]{:S(2)}) copy-start(bf16[640,512]{1,0:T(8,128)(2,1)} %cotangent_ref.1) | copy-start | bytes 1966084
  17.0 33.6 %copy-start.5 = (s32[8,640]{1,0:T(8,128)S(1)}, s32[8,640]{1,0:T(8,128)}, u32[]{:S(2)}) copy-start(s32[8,640]{1,0:T(8,128)} %get-tuple-element.12.place_ref) | copy-start | bytes 61444
  20.5 30.1 %copy-start = (bf16[512,2048]{1,0:T(8,128)(2,1)S(1)}, bf16[512,2048]{1,0:T(8,128)(2,1)}, u32[]{:S(2)}) copy-start(bf16[512,2048]{1,0:T(8,128)(2,1)} %w_ref.1) | copy-start | bytes 6291460
  20.5 30.1 %copy-start.4 = (bf16[512,512]{1,0:T(8,128)(2,1)S(1)}, bf16[512,512]{1,0:T(8,128)(2,1)}, u32[]{:S(2)}) copy-start(bf16[512,512]{1,0:T(8,128)(2,1)} %w_out_ref.1) | copy-start | bytes 1572868
  20.5 30.1 %copy-start.7 = (s32[1,640]{1,0:T(1,128)S(1)}, s32[1,640]{1,0:T(1,128)}, u32[]{:S(2)}) copy-start(s32[1,640]{1,0:T(1,128)} %segment_ref.1) | copy-start | bytes 7684
  87.7 9.8 %copy-start.2 = (f32[2048,64]{0,1:T(8,128)S(1)}, f32[2048,64]{0,1:T(8,128)}, u32[]{:S(2)}) copy-start(f32[2048,64]{0,1:T(8,128)} %param.8) | copy-start | bytes 1572868
  87.7 9.8 %copy-start.6 = (f32[2048]{0:T(1024)S(1)}, f32[2048]{0:T(1024)}, u32[]{:S(2)}) copy-start(f32[2048]{0:T(1024)} %param.9) | copy-start | bytes 24580
  90.6 2.1 %collective-permute-start = (f32[16,128]{1,0:T(8,128)S(1)}, f32[16,128]{1,0:T(8,128)S(1)}, u32[]{:S(2)}, u32[]{:S(2)}) collective-permute-start(f32[16,128]{1,0:T(8,128)S(1)} %get-tuple-element.15), channel_id=1, source_target_pairs={{0,1},{1,0},{2,3},{3,2},{4,5},{5,4},{6,7},{7,6},{8,9},{9,8},{10,11... | collective-permute-start | bytes 24584 | tf_op jit(solution)/shard_map/ppermute | solution.py:458
  92.8 3.7 %collective-permute-start.3 = (f32[16,128]{1,0:T(8,128)S(1)}, f32[16,128]{1,0:T(8,128)S(1)}, u32[]{:S(2)}, u32[]{:S(2)}) collective-permute-start(f32[16,128]{1,0:T(8,128)S(1)} %add.4.own_ref), channel_id=1, source_target_pairs={{0,6},{1,7},{2,4},{3,5},{4,2},{5,3},{6,0},{7,1},{8,14},{9,15},{10,... | collective-permute-start | bytes 24584 | tf_op jit(solution)/shard_map/ppermute | solution.py:458
  92.8 4.0 %collective-permute-start.2 = (f32[16,128]{1,0:T(8,128)S(1)}, f32[16,128]{1,0:T(8,128)S(1)}, u32[]{:S(2)}, u32[]{:S(2)}) collective-permute-start(f32[16,128]{1,0:T(8,128)S(1)} %add.4.own_ref), channel_id=1, source_target_pairs={{0,4},{1,5},{2,6},{3,7},{4,0},{5,1},{6,2},{7,3},{8,12},{9,13},{10,... | collective-permute-start | bytes 24584 | tf_op jit(solution)/shard_map/ppermute | solution.py:458
  94.6 2.9 %collective-permute-start.1 = (f32[16,128]{1,0:T(8,128)S(1)}, f32[16,128]{1,0:T(8,128)S(1)}, u32[]{:S(2)}, u32[]{:S(2)}) collective-permute-start(f32[16,128]{1,0:T(8,128)S(1)} %add.4.own_ref), channel_id=1, source_target_pairs={{0,2},{1,3},{2,0},{3,1},{4,6},{5,7},{6,4},{7,5},{8,10},{9,11},{10,... | collective-permute-start | bytes 24584 | tf_op jit(solution)/shard_map/ppermute | solution.py:458
